TPU v7x, 512 devices: a whole 4x4x16 slice. The times are simulated.
512 devices in a mesh: batch: 64 (over y, z), tile: 8 (over x, core).
Axes of the slice: x: 4, y: 4, z: 16, core: 2. Of those that a mesh axis runs over, the one named last changes fastest.
Arguments:
- first_view_output: bfloat16 [4096, 4096], P('batch', 'tile'), may hold values from -900 to 900
- second_view_output: bfloat16 [4096, 4096], P('batch', 'tile'), may hold values from -900 to 900
Outputs:
- gradient_first_view: bfloat16 [4096, 4096], P('batch', 'tile')
- gradient_second_view: bfloat16 [4096, 4096], P('batch', 'tile')
- loss: float32 [], replicated
All inputs are finite; a program needn't handle non-finite values.
Results may differ from a plain program's by a relative error of at most 0.0054.
Values may be sent and summed in bfloat16 or wider, within the bound.
A program may use at most 64 MiB of HBM per device.

v0:
```python
import jax
import jax.numpy as jnp
from jax import lax
from jax.sharding import PartitionSpec as P

epsilon = 1e-05
off_weight = 0.0051


def local(first_view_output, second_view_output):
    row_count, width_dev = first_view_output.shape
    batch_count = lax.axis_size("batch")
    tile_count = lax.axis_size("tile")
    overall_row_count = row_count * batch_count
    part_width = width_dev // batch_count
    band_width = part_width * tile_count
    full_width = width_dev * tile_count
    batch_index = lax.axis_index("batch")
    tile_index = lax.axis_index("tile")
    wide_one = first_view_output.astype(jnp.float32)
    wide_two = second_view_output.astype(jnp.float32)
    first_sums = lax.psum((jnp.sum(wide_one, axis=0), jnp.sum(wide_two, axis=0)), "batch")
    centered_first_view = wide_one - first_sums[0] / overall_row_count
    centered_second_view = wide_two - first_sums[1] / overall_row_count
    second_sums = lax.psum(
        (
            jnp.sum(centered_first_view * centered_first_view, axis=0),
            jnp.sum(centered_second_view * centered_second_view, axis=0),
        ),
        "batch",
    )
    spread_one = second_sums[0] / overall_row_count
    spread_two = second_sums[1] / overall_row_count
    inverse_deviation_first = lax.rsqrt(spread_one + epsilon)
    inverse_deviation_second = lax.rsqrt(spread_two + epsilon)
    standardized_first = centered_first_view * inverse_deviation_first
    standardized_second = centered_second_view * inverse_deviation_second
    normed_first_view = standardized_first.astype(jnp.bfloat16)
    normed_second_view = standardized_second.astype(jnp.bfloat16)
    received = lax.all_to_all(
        normed_second_view.reshape(row_count, batch_count, part_width),
        "batch",
        split_axis=1,
        concat_axis=0,
        tiled=True,
    )
    tile_columns = lax.all_gather(
        received.reshape(overall_row_count, part_width), "tile", axis=1, tiled=True
    )
    matching = tile_columns
    correlation = (
        lax.dot_general(
            lax.all_gather(normed_first_view, "batch", axis=0, tiled=True),
            matching,
            (((0,), (0,)), ((), ())),
            preferred_element_type=jnp.float32,
        )
        / overall_row_count
    )
    row_ids = tile_index * width_dev + jnp.arange(width_dev, dtype=jnp.int32)[:, None]
    column_pos = jnp.arange(band_width, dtype=jnp.int32)
    column_ids = (
        column_pos // part_width * width_dev + batch_index * part_width + column_pos % part_width
    )
    on_diagonal = row_ids == column_ids[None, :]
    local_loss = jnp.sum(
        jnp.where(
            on_diagonal,
            (1.0 - correlation) * (1.0 - correlation),
            off_weight * correlation * correlation,
        )
    )
    loss = lax.psum(local_loss, ("batch", "tile")) / full_width
    grad_tile = jnp.where(
        on_diagonal, -2.0 * (1.0 - correlation), 2.0 * off_weight * correlation
    ).astype(jnp.bfloat16)
    full_one, full_two = (
        lax.all_gather(normed_first_view, "tile", axis=1, tiled=True),
        lax.all_gather(normed_second_view, "tile", axis=1, tiled=True),
    )
    reordered_two = (
        full_two.reshape(row_count, tile_count, batch_count, part_width)
        .transpose(0, 2, 1, 3)
        .reshape(row_count, full_width)
    )
    matching = reordered_two
    backward_first_view = lax.dot_general(
        matching,
        lax.all_gather(grad_tile, "batch", axis=1, tiled=True),
        (((1,), (1,)), ((), ())),
        preferred_element_type=jnp.float32,
    )
    column_parts = lax.all_to_all(
        grad_tile.reshape(width_dev, tile_count, part_width),
        "tile",
        split_axis=1,
        concat_axis=0,
        tiled=True,
    ).reshape(full_width, part_width)
    backward_second_view = jnp.dot(
        full_one,
        lax.all_gather(column_parts, "batch", axis=1, tiled=True),
        preferred_element_type=jnp.float32,
    )
    backward_column_totals = lax.psum(
        (
            jnp.sum(backward_first_view, axis=0),
            jnp.sum(backward_first_view * standardized_first, axis=0),
            jnp.sum(backward_second_view, axis=0),
            jnp.sum(backward_second_view * standardized_second, axis=0),
        ),
        "batch",
    )
    gradient_first_view = (
        (
            backward_first_view
            - backward_column_totals[0] / overall_row_count
            - standardized_first * (backward_column_totals[1] / overall_row_count)
        )
        * inverse_deviation_first
    ).astype(jnp.bfloat16)
    gradient_second_view = (
        (
            backward_second_view
            - backward_column_totals[2] / overall_row_count
            - standardized_second * (backward_column_totals[3] / overall_row_count)
        )
        * inverse_deviation_second
    ).astype(jnp.bfloat16)
    return (gradient_first_view, gradient_second_view, loss)


def solution(mesh):
    placed = (P("batch", "tile"), P("batch", "tile"))
    return jax.shard_map(
        local,
        mesh=mesh,
        in_specs=placed,
        out_specs=(P("batch", "tile"), P("batch", "tile"), P()),
        check_vma=False,
    )
```

profile of v0, /device:TPU:2, one launch (start us, length us, event | category | flops | bytes accessed | tf_op | source)
XLA Modules:
  0.0 881.6 jit_solution(16513748007691336689)
XLA Ops:
  7.2 0.0 all-gather.4.cloned.1.call-start
  7.2 0.9 convert_reduce_fusion.1
  8.1 0.9 convert_reduce_fusion
  8.9 149.9 %all-reduce.2 = (f32[512]{0:T(512)S(1)}, f32[512]{0:T(512)S(1)}) all-reduce(f32[512]{0:T(512)S(1)} %convert_reduce_fusion.1, f32[512]{0:T(512)S(1)} %convert_reduce_fusion), channel_id=1, replica_groups=mesh['batch'=64,'tile'=8] {'batch'}, use_global_device_ids=true, to_apply=%region_1.0 | all-reduce | flops 1024 | bytes 8192 | tf_op jit(solution)/shard_map/psum | solution.py:22
  158.8 0.9 fusion.19
  159.7 0.9 fusion.14
  160.6 138.0 %all-reduce.1 = (f32[512]{0:T(512)S(1)}, f32[512]{0:T(512)S(1)}) all-reduce(f32[512]{0:T(512)S(1)} %fusion.19, f32[512]{0:T(512)S(1)} %fusion.14), channel_id=1, replica_groups=mesh['batch'=64,'tile'=8] {'batch'}, use_global_device_ids=true, to_apply=%region_3.0 | all-reduce | flops 1024 | bytes 8192 | tf_op jit(solution)/shard_map/psum | solution.py:25
  298.6 1.5 fusion.9
  300.1 0.0 all-gather.4.cloned.1.call-update
  300.1 0.9 fusion.4
  301.0 0.1 copy.7
  301.1 0.8 reshape.68
  301.9 4.6 all-to-all-start
  306.5 0.0 all-gather.6.cloned.1.call-start
  306.6 14.6 %all-to-all-done = bf16[64,2,256]{2,1,0:T(2,128)(2,1)S(1)} async-done(((bf16[64,2,256]{2,1,0:T(2,128)(2,1)}), bf16[64,2,256]{2,1,0:T(2,128)(2,1)S(1)}, u32[]{:S(2)}, u32[]{:S(2)}) %all-to-all-start) | async-done | bytes 65568 | tf_op jit(solution)/shard_map/all_to_all | solution.py:40
  321.2 0.1 reshape.69
  321.4 0.2 reshape.65
  321.6 13.1 %all_gather.20 = bf16[4096,64]{0,1:T(8,128)(2,1)S(1)} all-gather(bf16[4096,8]{0,1:T(8,128)(2,1)S(1)} %reshape.65), channel_id=1, replica_groups=mesh['batch'=64,'tile'=8] {'tile'}, dimensions={1}, use_global_device_ids=true | all-gather | bytes 589824 | tf_op jit(solution)/shard_map/all_gather | solution.py:47
  334.7 0.0 copy-start.2
  334.7 0.0 copy-start
  334.8 102.3 %all-gather.4.cloned.1.call-done = bf16[4096,512]{1,0:T(8,128)(2,1)} async-done(((bf16[64,512]{1,0:T(8,128)(2,1)}), bf16[4096,512]{1,0:T(8,128)(2,1)}) %all-gather.4.cloned.1.call-update) | async-done | bytes 4194320 | tf_op jit(solution)/shard_map/all_gather | solution.py:53
  437.0 4.3 fusion.21
  441.3 0.0 all-gather.6.cloned.1.call-update
  441.3 0.0 all-gather.8.cloned.1.call-start
  441.4 9.1 %all_to_all.30 = bf16[512,8,8]{0,2,1:T(8,128)(2,1)} all-to-all(bf16[512,8,8]{0,2,1:T(8,128)(2,1)} %bitcast.32), channel_id=1, replica_groups=mesh['batch'=64,'tile'=8] {'tile'}, dimensions={1} | all-to-all | bytes 131072 | tf_op jit(solution)/shard_map/all_to_all | solution.py:93
  450.5 0.0 all-gather.8.cloned.1.call-update
  450.5 12.5 %all_gather.18 = bf16[64,4096]{1,0:T(8,128)(2,1)S(1)} all-gather(bf16[64,512]{1,0:T(8,128)(2,1)S(1)} %fusion.4), channel_id=1, replica_groups=mesh['batch'=64,'tile'=8] {'tile'}, dimensions={1}, use_global_device_ids=true | all-gather | bytes 589824 | tf_op jit(solution)/shard_map/all_gather | solution.py:79
  463.0 0.5 copy.5
  463.5 0.0 copy-start.1
  463.5 0.3 copy.6
  463.8 0.0 copy-done.2
  463.8 13.1 %all_gather.22 = bf16[64,4096]{1,0:T(8,128)(2,1)S(1)} all-gather(bf16[64,512]{1,0:T(8,128)(2,1)S(1)} %copy-done.2), channel_id=1, replica_groups=mesh['batch'=64,'tile'=8] {'tile'}, dimensions={1}, use_global_device_ids=true | all-gather | bytes 589824 | tf_op jit(solution)/shard_map/all_gather | solution.py:78
  476.9 101.6 %psum.71 = f32[]{:T(128)} all-reduce(f32[]{:T(128)} %get-tuple-element.15), channel_id=1, replica_groups=mesh['batch'=64,'tile'=8] {'batch','tile'}, use_global_device_ids=true, to_apply=%region_17.18 | all-reduce | flops 1 | bytes 8 | tf_op jit(solution)/shard_map/psum | solution.py:73
  579.2 3.0 all-gather.6.cloned.1.call-done
  582.3 0.0 copy-done
  582.3 3.1 fusion.26
  585.3 141.2 %all-gather.8.cloned.1.call-done = bf16[4096,512]{0,1:T(8,128)(2,1)} async-done(((bf16[4096,8]{0,1:T(8,128)(2,1)}), bf16[4096,512]{0,1:T(8,128)(2,1)}) %all-gather.8.cloned.1.call-update) | async-done | bytes 4194320 | tf_op jit(solution)/shard_map/all_gather | solution.py:102
  726.6 0.0 copy-done.1
  726.6 3.6 fusion.25
  730.2 142.4 %all-reduce = (f32[512]{0:T(512)S(1)}, f32[512]{0:T(512)S(1)}, f32[512]{0:T(512)S(1)}, f32[512]{0:T(512)S(1)}) all-reduce(f32[512]{0:T(512)S(1)} %get-tuple-element.6, f32[512]{0:T(512)S(1)} %get-tuple-element.5, f32[512]{0:T(512)S(1)} %get-tuple-element.4, f32[512]{0:T(512)S(1)} %get-tuple-element.3), channel_id=1, replica_groups=mesh['batch'=64,'tile'=8] {'batch'}, use_global_device_ids=true, to_apply=%region_11.12 | all-reduce | flops 2048 | bytes 16384 | tf_op jit(solution)/shard_map/psum | solution.py:105
  872.6 0.7 fusion.13
  873.3 0.7 fusion.18
  (12 shorter events, 0.1 us)
Async XLA Ops:
  7.2 429.9 %all-gather.4.cloned.1.call-start = ((), (), s32[]{:S(2)}) async-start(), calls=%async_computation.2 | async-start | bytes 4259840 | tf_op jit(solution)/shard_map/all_gather | solution.py:53
  301.9 19.3 %all-to-all-start = ((bf16[64,2,256]{2,1,0:T(2,128)(2,1)}), bf16[64,2,256]{2,1,0:T(2,128)(2,1)S(1)}, u32[]{:S(2)}, u32[]{:S(2)}) async-start(bf16[64,2,256]{2,1,0:T(2,128)(2,1)} %reshape.68), calls=%async_computation | async-start | bytes 131072 | tf_op jit(solution)/shard_map/all_to_all | solution.py:40
  306.5 275.7 %all-gather.6.cloned.1.call-start = ((), (), s32[]{:S(2)}) async-start(), calls=%async_computation.3 | async-start | bytes 4259840 | tf_op jit(solution)/shard_map/all_gather | solution.py:89
  334.7 129.1 %copy-start.2 = (bf16[64,512]{1,0:T(8,128)(2,1)S(1)}, bf16[64,512]{1,0:T(8,128)(2,1)}, u32[]{:S(2)}) copy-start(bf16[64,512]{1,0:T(8,128)(2,1)} %fusion.9) | copy-start | bytes 196612
  334.7 247.5 %copy-start = (bf16[64,512]{1,0:T(8,128)(2,1)S(1)}, bf16[64,512]{1,0:T(8,128)(2,1)}, u32[]{:S(2)}) copy-start(bf16[64,512]{1,0:T(8,128)(2,1)} %param.2) | copy-start | bytes 196612
  441.3 285.2 %all-gather.8.cloned.1.call-start = ((), (), s32[]{:S(2)}) async-start(), calls=%async_computation.4 | async-start | bytes 4259840 | tf_op jit(solution)/shard_map/all_gather | solution.py:102
  463.5 263.1 %copy-start.1 = (bf16[64,512]{1,0:T(8,128)(2,1)S(1)}, bf16[64,512]{1,0:T(8,128)(2,1)}, u32[]{:S(2)}) copy-start(bf16[64,512]{1,0:T(8,128)(2,1)} %param.3) | copy-start | bytes 196612
Sparse Core Ops, SparseCore 0:
  300.2 136.7 all-gather.3
  441.5 140.7 all-gather.5
  585.2 141.3 all-gather.7
where the time goes:
time: 882 us
  blocking collectives  580 us (66%)
  waiting for transfers between devices  261 us (30%)
  between operations  15.7 us (2%)
  matrix products  10.9 us (1%)
    psum x1, blocking collectives, local(): lax.psum((jnp.sum(wide_one, axis=0), jnp.sum(wide_two, axis=0)), 'batch')  150 us
    psum x1, blocking collectives, local(): lax.psum((jnp.sum(backward_first_view, axis=0), jnp.sum(backward_first_vi...  142 us
    all_gather x1, waiting for transfers between devices, local(): lax.all_gather(column_parts, 'batch', axis=1, tiled=True)  141 us
    psum x1, blocking collectives, local(): lax.psum((jnp.sum(centered_first_view * centered_first_view, axis=0), jnp...  138 us
    all_gather x1, waiting for transfers between devices, local(): lax.all_gather(normed_first_view, 'batch', axis=0, tiled=True)  102 us
    psum x1, blocking collectives, local(): loss = lax.psum(local_loss, ('batch', 'tile')) / full_width  102 us
  transfers between devices with their start and end apart: 4, of which 4 were waited for; matrix products, arithmetic and copies ran while one was open for 1% of the time, Pallas kernels for 0%

commit v1 on v0

v1 whole, which is shorter than its diff:
```python
import jax
import jax.numpy as jnp
from jax import lax
from jax.experimental import pallas as pl
from jax.experimental.pallas import tpu as pltpu
from jax.sharding import PartitionSpec as P

epsilon = 1e-05
off_weight = 0.0051
SIDE = 4
DEPTH = 16
ROWS = 64
LANE = 128
MESH = pl.DeviceIdType.MESH


def kernel(
    x1, x2, o1, o2, loss_ref,
    stage, gath, nbuf, oth, stat, cross, tail, coef,
    ksend, arecv, bsend, brecv, csend, kfull, acc, gout, outs, lbx, lby,
    ssem, misc, grecv, asem, bsem, csem, dsem,
):
    n, nz, rows = SIDE, DEPTH, ROWS
    group = n * rows
    width = 2 * LANE
    apiece, bpiece = group // n, group // (n * n)
    half = nz // 2
    features = float(n * n * width)
    b, t = lax.axis_index("batch"), lax.axis_index("tile")
    y, z = b // nz, lax.rem(b, nz)
    x, c = t // 2, lax.rem(t, 2)

    def dev(x, c, y, z):
        return (y * nz + z, x * 2 + c)

    def xp(d):
        return lax.rem(x + d, n)

    def yp(d):
        return lax.rem(y + d, n)

    def zp(d):
        return lax.rem(z + d + nz, nz)

    def send(src, dst, out, into, to):
        pltpu.make_async_remote_copy(
            src_ref=src, dst_ref=dst, send_sem=out, recv_sem=into,
            device_id=to, device_id_type=MESH,
        ).start()

    def arrive(ref, sem):
        pltpu.make_async_copy(ref, ref, sem).wait()

    barrier = pltpu.get_barrier_semaphore()
    peers = 0
    for dc in range(2):
        for d in range(n):
            if d or dc:
                cc = lax.rem(c + dc, 2)
                pl.semaphore_signal(barrier, 1, device_id=dev(x, cc, yp(d), z), device_id_type=MESH)
                peers += 1
            if d:
                cc = lax.rem(c + dc, 2)
                pl.semaphore_signal(barrier, 1, device_id=dev(xp(d), cc, y, z), device_id_type=MESH)
                peers += 1
    for d in range(1, nz):
        pl.semaphore_signal(barrier, 1, device_id=dev(x, c, y, zp(d)), device_id_type=MESH)
        peers += 1
    for q in range(n):
        stage[0, q] = x1[:, q * LANE:(q + 1) * LANE]
        stage[1, q] = x2[:, q * LANE:(q + 1) * LANE]
    acc[...] = jnp.zeros_like(acc)
    pl.semaphore_wait(barrier, peers)

    for dc in range(2):
        for d in range(n):
            if d or dc:
                v, yy = lax.rem(c + dc, 2), yp(d)
                send(stage.at[v, yy], gath.at[z, c * n + y], ssem.at[0], misc.at[0], dev(x, v, yy, z))
    gath[z, c * n + y] = stage[c, y]
    arrive(gath.at[z, pl.ds(0, 2 * n - 1)], misc.at[0])

    def block_of(way, s):
        return zp(-s) if way == 0 else zp(s)

    def forward(way, s, h):
        part = gath.at[block_of(way, s), pl.ds(h * n, n)]
        to = zp(1) if way == 0 else zp(-1)
        send(part, part, ssem.at[1], grecv.at[way, s, h], dev(x, c, y, to))

    for h in range(2):
        for way in range(2):
            forward(way, 0, h)

    def centre(block, h, q):
        return gath[block, h * n + q].astype(jnp.float32)

    for h in range(2):
        cols = slice(h * LANE, (h + 1) * LANE)
        total = jnp.zeros((1, LANE), jnp.float32)
        for q in range(n):
            total += jnp.sum(centre(z, h, q), axis=0, keepdims=True)
        mean = total / group
        spread = jnp.zeros((1, LANE), jnp.float32)
        for q in range(n):
            v = centre(z, h, q) - mean
            spread += jnp.sum(v * v, axis=0, keepdims=True)
        stat[z, 0:1, cols] = mean
        stat[z, 1:2, cols] = spread
    for d in range(1, nz):
        send(stat.at[z], stat.at[z], ssem.at[2], misc.at[1], dev(x, c, y, zp(d)))
    arrive(stat.at[pl.ds(0, nz - 1)], misc.at[1])
    mean = jnp.zeros((1, width), jnp.float32)
    for q in range(nz):
        mean += stat[q, 0:1, :]
    mean = mean / nz
    spread = jnp.zeros((1, width), jnp.float32)
    for q in range(nz):
        v = stat[q, 0:1, :] - mean
        spread += stat[q, 1:2, :] + group * (v * v)
    coef[0:1, :] = mean
    coef[1:2, :] = lax.rsqrt(spread / (group * nz) + epsilon)

    def standard(block, h, q):
        cols = slice(h * LANE, (h + 1) * LANE)
        return (centre(block, h, q) - coef[0:1, cols]) * coef[1:2, cols]

    def normalize(block):
        for h in range(2):
            for q in range(n):
                nbuf[block, q * rows:(q + 1) * rows, h * LANE:(h + 1) * LANE] = standard(
                    block, h, q
                ).astype(jnp.bfloat16)

    normalize(z)
    send(nbuf.at[z], oth, ssem.at[3], misc.at[2], dev(x, 1 - c, y, z))

    def peer(axis, d, cc):
        return dev(xp(d), cc, y, z) if axis == 0 else dev(x, cc, yp(d), z)

    def step(i, carry):
        for h in range(2):
            for way in range(2):
                last = half if h == way else half - 1

                @pl.when((i >= 1) & (i <= last))
                def _():
                    arrive(gath.at[block_of(way, i), pl.ds(h * n, n)], grecv.at[way, i - 1, h])

                @pl.when((i >= 1) & (i <= last - 1))
                def _():
                    forward(way, i, h)

        for k in range(2):
            first, second = (0, 1) if k == 0 else (1, 0)
            at_first, at_second = (x, y) if k == 0 else (y, x)

            j = i - k

            @pl.when((j >= 0) & (j < half))
            def _():
                block = block_of(k, i)

                @pl.when(i > 0)
                def _():
                    normalize(block)

                ksend[k, j] = lax.dot_general(
                    nbuf[z], nbuf[block], (((1,), (1,)), ((), ())),
                    preferred_element_type=jnp.float32,
                ).astype(jnp.bfloat16).reshape(n, apiece, group)
                for d in range(1, n):
                    to = lax.rem(at_first + d, n)
                    send(ksend.at[k, j, to], arecv.at[k, j, d - 1], ssem.at[4], asem.at[k, j], peer(first, d, c))

            j1 = i - k - 1

            @pl.when((j1 >= 0) & (j1 < half))
            def _():
                arrive(arecv.at[k, j1], asem.at[k, j1])
                s = ksend[k, j1, at_first].astype(jnp.float32)
                for d in range(n - 1):
                    s += arecv[k, j1, d].astype(jnp.float32)
                bsend[k, j1] = s.astype(jnp.bfloat16).reshape(n, bpiece, group)
                for d in range(1, n):
                    to = lax.rem(at_second + d, n)
                    send(bsend.at[k, j1, to], brecv.at[k, j1, d - 1], ssem.at[5], bsem.at[k, j1], peer(second, d, c))

            j2 = i - k - 2

            @pl.when((j2 >= 0) & (j2 < half))
            def _():
                arrive(brecv.at[k, j2], bsem.at[k, j2])
                s = bsend[k, j2, at_second].astype(jnp.float32)
                for d in range(n - 1):
                    s += brecv[k, j2, d].astype(jnp.float32)
                csend[k, j2] = s.astype(jnp.bfloat16)
                for d in range(n):
                    send(csend.at[k, j2], kfull.at[k, j2, at_first, at_second], ssem.at[6], csem.at[k, j2], peer(second, d, 1 - c))

            j3 = i - k - 3

            @pl.when((j3 >= 0) & (j3 < half))
            def _():
                arrive(kfull.at[k, j3, at_first], csem.at[k, j3])
                for d in range(1, n):
                    send(kfull.at[k, j3, at_first], kfull.at[k, j3, at_first], ssem.at[7], dsem.at[k, j3], peer(first, d, c))

            j4 = i - k - 4

            @pl.when((j4 >= 0) & (j4 < half))
            def _():
                arrive(arecv.at[k, j4], dsem.at[k, j4])
                acc[...] += jnp.dot(
                    kfull[k, j4].reshape(group, group), nbuf[block_of(k, i - 4)],
                    preferred_element_type=jnp.float32,
                )

        @pl.when(i == 2)
        def _():
            arrive(oth, misc.at[2])
            for h in range(2):
                cols = slice(h * LANE, (h + 1) * LANE)
                sums = [jnp.zeros((1, LANE), jnp.float32)] * 3
                for q in range(n):
                    lines = slice(q * rows, (q + 1) * rows)
                    theirs = oth[lines, cols].astype(jnp.float32)
                    ours = nbuf[z, lines, cols].astype(jnp.float32)
                    for m, v in enumerate((theirs, theirs * standard(z, h, q), theirs * ours)):
                        sums[m] = sums[m] + jnp.sum(v, axis=0, keepdims=True)
                for m in range(3):
                    cross[z, m:m + 1, cols] = sums[m]
                cross[z, 3:4, cols] = jnp.zeros((1, LANE), jnp.float32)
            for d in range(1, nz):
                send(cross.at[z], cross.at[z], ssem.at[8], misc.at[3], dev(x, c, y, zp(d)))

        return carry

    lax.fori_loop(0, half + 5, step, 0)

    for h in range(2):
        cols = slice(h * LANE, (h + 1) * LANE)
        plain = jnp.zeros((1, LANE), jnp.float32)
        times = jnp.zeros((1, LANE), jnp.float32)
        for q in range(n):
            v = acc[q * rows:(q + 1) * rows, cols]
            plain += jnp.sum(v, axis=0, keepdims=True)
            times += jnp.sum(v * standard(z, h, q), axis=0, keepdims=True)
        tail[z, 0:1, cols] = plain
        tail[z, 1:2, cols] = times
    for d in range(1, nz):
        send(tail.at[z], tail.at[z], ssem.at[9], misc.at[4], dev(x, c, y, zp(d)))
    arrive(cross.at[pl.ds(0, nz - 1)], misc.at[3])
    mixed = cross[0]
    for q in range(1, nz):
        mixed += cross[q]
    total_rows = float(group * nz)
    mixed = mixed / total_rows
    diagonal = mixed[2:3, :]
    scale = 2.0 * off_weight / total_rows
    lead = -2.0 * (1.0 - diagonal) - 2.0 * off_weight * diagonal
    arrive(tail.at[pl.ds(0, nz - 1)], misc.at[4])
    sums = tail[0]
    for q in range(1, nz):
        sums += tail[q]
    sums = sums / total_rows
    coef[2:3, :] = lead
    coef[3:4, :] = scale * sums[0:1, :] + lead * mixed[0:1, :]
    coef[4:5, :] = scale * sums[1:2, :] + lead * mixed[1:2, :]

    terms = (1.0 - diagonal) * (1.0 - diagonal) + off_weight * (
        sums[1:2, :] / total_rows - diagonal * diagonal
    )
    mine = jnp.sum(terms, axis=1, keepdims=True) * (0.5 / features)
    lbx[t] = jnp.broadcast_to(mine, (1, LANE))
    for dc in range(2):
        for d in range(n):
            if d:
                send(lbx.at[t], lbx.at[t], ssem.at[10], misc.at[5], dev(xp(d), lax.rem(c + dc, 2), y, z))
    send(lbx.at[t], lbx.at[t], ssem.at[10], misc.at[5], dev(x, 1 - c, y, z))

    for h in range(2):
        cols = slice(h * LANE, (h + 1) * LANE)
        for q in range(n):
            lines = slice(q * rows, (q + 1) * rows)
            back = scale * acc[lines, cols] + coef[2:3, cols] * oth[lines, cols].astype(jnp.float32)
            g = (back - coef[3:4, cols] - standard(z, h, q) * coef[4:5, cols]) * coef[1:2, cols]
            gout[h * n + q] = g.astype(jnp.bfloat16)
    for dc in range(2):
        for d in range(n):
            if d or dc:
                v, yy = lax.rem(c + dc, 2), yp(d)
                send(gout.at[v * n + yy], outs.at[c, y], ssem.at[11], misc.at[6], dev(x, v, yy, z))
    outs[c, y] = gout[c * n + y]

    arrive(lbx.at[pl.ds(0, 2 * n - 1)], misc.at[5])
    part = lbx[0]
    for q in range(1, 2 * n):
        part += lbx[q]
    lby[y] = part
    for d in range(1, n):
        send(lby.at[y], lby.at[y], ssem.at[12], misc.at[7], dev(x, c, yp(d), z))

    arrive(gath.at[0, pl.ds(0, 2 * n - 1)], misc.at[6])
    for q in range(n):
        o1[:, q * LANE:(q + 1) * LANE] = outs[0, q]
        o2[:, q * LANE:(q + 1) * LANE] = outs[1, q]
    arrive(lby.at[pl.ds(0, n - 1)], misc.at[7])
    part = lby[0]
    for q in range(1, n):
        part += lby[q]
    loss_ref[...] = part

    arrive(gath.at[0, pl.ds(0, 2 * n - 1)], ssem.at[0])
    arrive(gath.at[pl.ds(0, nz - 1)], ssem.at[1])
    arrive(stat.at[pl.ds(0, nz - 1)], ssem.at[2])
    arrive(oth, ssem.at[3])
    arrive(arecv, ssem.at[4])
    arrive(brecv, ssem.at[5])
    arrive(bsend, ssem.at[6])
    arrive(arecv, ssem.at[7])
    arrive(cross.at[pl.ds(0, nz - 1)], ssem.at[8])
    arrive(tail.at[pl.ds(0, nz - 1)], ssem.at[9])
    arrive(lbx.at[pl.ds(0, 2 * n - 1)], ssem.at[10])
    arrive(gath.at[0, pl.ds(0, 2 * n - 1)], ssem.at[11])
    arrive(lby.at[pl.ds(0, n - 1)], ssem.at[12])


def local(first_view_output, second_view_output):
    n, nz, rows = SIDE, DEPTH, ROWS
    group, width, half = n * rows, 2 * LANE, nz // 2
    apiece, bpiece = group // n, group // (n * n)
    bf16, f32 = jnp.bfloat16, jnp.float32
    shape = first_view_output.shape
    vmem = pl.BlockSpec(memory_space=pltpu.VMEM)
    g1, g2, loss = pl.pallas_call(
        kernel,
        out_shape=(
            jax.ShapeDtypeStruct(shape, bf16),
            jax.ShapeDtypeStruct(shape, bf16),
            jax.ShapeDtypeStruct((1, LANE), f32),
        ),
        in_specs=[vmem] * 2,
        out_specs=(vmem,) * 3,
        scratch_shapes=[
            pltpu.VMEM((2, n, rows, LANE), bf16),
            pltpu.VMEM((nz, 2 * n, rows, LANE), bf16),
            pltpu.VMEM((nz, group, width), bf16),
            pltpu.VMEM((group, width), bf16),
            pltpu.VMEM((nz, 2, width), f32),
            pltpu.VMEM((nz, 4, width), f32),
            pltpu.VMEM((nz, 2, width), f32),
            pltpu.VMEM((8, width), f32),
            pltpu.VMEM((2, half, n, apiece, group), bf16),
            pltpu.VMEM((2, half, n - 1, apiece, group), bf16),
            pltpu.VMEM((2, half, n, bpiece, group), bf16),
            pltpu.VMEM((2, half, n - 1, bpiece, group), bf16),
            pltpu.VMEM((2, half, bpiece, group), bf16),
            pltpu.VMEM((2, half, n, n, bpiece, group), bf16),
            pltpu.VMEM((group, width), f32),
            pltpu.VMEM((2 * n, rows, LANE), bf16),
            pltpu.VMEM((2, n, rows, LANE), bf16),
            pltpu.VMEM((2 * n, 1, LANE), f32),
            pltpu.VMEM((n, 1, LANE), f32),
            pltpu.SemaphoreType.DMA((13,)),
            pltpu.SemaphoreType.DMA((8,)),
            pltpu.SemaphoreType.DMA((2, half, 2)),
            pltpu.SemaphoreType.DMA((2, half)),
            pltpu.SemaphoreType.DMA((2, half)),
            pltpu.SemaphoreType.DMA((2, half)),
            pltpu.SemaphoreType.DMA((2, half)),
        ],
        compiler_params=pltpu.CompilerParams(
            collective_id=0, has_side_effects=True, vmem_limit_bytes=40 * 2**20
        ),
    )(first_view_output, second_view_output)
    return g1, g2, loss[0, 0]


def solution(mesh):
    spec = P("batch", "tile")
    return jax.shard_map(
        local, mesh=mesh, in_specs=(spec, spec), out_specs=(spec, spec, P()), check_vma=False
    )
```

time: 882 us -> 101 us (0.11)
  the two profiles are of different devices: /device:TPU:2 before, /device:TPU:1 now
where the time goes in v1:
time: 101 us; the launch traced here: 100 us
  Pallas kernels  95.6 us (95%)
  local copies, waits for them, and re-layouts  2.93 us (3%)
  between operations  1.81 us (2%)
    pallas_call x1, Pallas kernels, local(): pl.pallas_call(kernel, out_shape=(jax.ShapeDtypeStruct(shape, bf16), jax....  95.6 us
    unnamed x6, local copies, waits for them, and re-layouts  2.93 us

profile of v1, /device:TPU:1, one launch (start us, length us, event | category | flops | bytes accessed | tf_op | source)
XLA Modules:
  0.0 100.4 jit_solution(3239148906088383813)
XLA Ops:
  0.6 0.0 copy-start
  0.6 0.8 copy-done
  1.5 0.0 copy-start.1
  1.5 0.8 copy-done.1
  2.3 95.6 %shard_map.49 = (bf16[64,512]{1,0:T(8,128)(2,1)S(1)}, bf16[64,512]{1,0:T(8,128)(2,1)S(1)}, f32[1,128]{1,0:T(1,128)S(1)}) custom-call(bf16[64,512]{1,0:T(8,128)(2,1)S(1)} %copy-done, bf16[64,512]{1,0:T(8,128)(2,1)S(1)} %copy-done.1), custom_call_target="tpu_custom_call" | custom-call | tf_op jit(solution)/shard_map/pallas_call | solution.py:336
  97.9 0.6 copy.8
  98.6 0.6 copy.9
Async XLA Ops:
  0.6 0.8 copy-start
  1.5 0.8 copy-start.1

commit v2 on v0

v2 whole, which is shorter than its diff:
```python
import jax
import jax.numpy as jnp
from jax import lax
from jax.experimental import pallas as pl
from jax.experimental.pallas import tpu as pltpu
from jax.sharding import PartitionSpec as P

epsilon = 1e-05
off_weight = 0.0051
SIDE = 4
DEPTH = 16
ROWS = 64
COLS = 512
LANE = 128
LAG = 3
RING = 5
MESH = pl.DeviceIdType.MESH
f32, bf16 = jnp.float32, jnp.bfloat16


def kernel(
    x1, x2, o1, o2, loss_ref,
    own, gath, lraw, nl, nr, stl, sty, stz, mr, coef,
    ksend, arecv, dsend, kfull, acc, tl, ty, ysend, yrecv, total, gout, outs, lbx,
    ssem, misc, grecv, asem, dsem,
):
    n, nz, rows = SIDE, DEPTH, ROWS
    hr = rows // 2
    group = n * rows
    width = 2 * COLS
    half = nz // 2
    all_rows = float(group * nz)
    features = float(n * width)
    b, t = lax.axis_index("batch"), lax.axis_index("tile")
    y, z = b // nz, lax.rem(b, nz)
    x, c = t // 2, lax.rem(t, 2)

    def dev(x, c, y, z):
        return (y * nz + z, x * 2 + c)

    def xp(d):
        return lax.rem(x + d, n)

    def yp(d):
        return lax.rem(y + d, n)

    def zp(d):
        return lax.rem(z + d + nz, nz)

    def send(src, dst, out, into, to):
        pltpu.make_async_remote_copy(
            src_ref=src, dst_ref=dst, send_sem=out, recv_sem=into,
            device_id=to, device_id_type=MESH,
        ).start()

    def arrive(ref, sem):
        pltpu.make_async_copy(ref, ref, sem).wait()

    far = sorted(range(1, nz), key=lambda d: -min(d, nz - d))

    barrier = pltpu.get_barrier_semaphore()
    peers = 0
    for d in far:
        pl.semaphore_signal(barrier, 1, device_id=dev(x, c, y, zp(d)), device_id_type=MESH)
        peers += 1
    for dc in range(2):
        for d in range(n):
            cc = lax.rem(c + dc, 2)
            if d or dc:
                pl.semaphore_signal(barrier, 1, device_id=dev(x, cc, yp(d), z), device_id_type=MESH)
                peers += 1
            if d:
                pl.semaphore_signal(barrier, 1, device_id=dev(xp(d), cc, y, z), device_id_type=MESH)
                peers += 1

    for r in range(2):
        lines = slice(r * hr, (r + 1) * hr)
        own[0, c, r] = x1[lines, :]
        own[1, c, r] = x2[lines, :]
        gath[z, 2 * c + r] = own[c, c, r]
    for q in range(n):
        cols = slice(q * LANE, (q + 1) * LANE)
        v1, v2 = x1[:, cols].astype(f32), x2[:, cols].astype(f32)
        a1 = jnp.sum(v1, axis=0, keepdims=True) / rows
        a2 = jnp.sum(v2, axis=0, keepdims=True) / rows
        v1, v2 = v1 - a1, v2 - a2
        stl[q, 0:1, :] = a1
        stl[q, 1:2, :] = a2
        stl[q, 2:3, :] = jnp.sum(v1 * v1, axis=0, keepdims=True)
        stl[q, 3:4, :] = jnp.sum(v2 * v2, axis=0, keepdims=True)
        stl[q, 4:5, :] = jnp.sum(v1 * v2, axis=0, keepdims=True)
        stl[q, 5:8, :] = jnp.zeros((3, LANE), f32)
    sty[y] = stl[y]
    acc[...] = jnp.zeros_like(acc)
    pl.semaphore_wait(barrier, peers)

    for v in range(2):
        send(own.at[v, c], own.at[v, c], ssem.at[0], misc.at[0], dev(x, 1 - c, y, z))
    for d in range(1, n):
        send(stl.at[yp(d)], sty.at[y], ssem.at[1], misc.at[1], dev(x, c, yp(d), z))

    def block_of(way, s):
        return zp(-s) if way == 0 else zp(s)

    def piece(i):
        return lax.rem(2 * c + i, 4)

    def forward(way, s, i):
        part = gath.at[block_of(way, s), piece(i)]
        to = zp(1) if way == 0 else zp(-1)
        send(part, part, ssem.at[2], grecv.at[way, s, i], dev(x, c, y, to))

    def ring(s, pieces):
        for i in pieces:
            for way in range(2):
                last = half if i // 2 == way else half - 1

                @pl.when(s <= last)
                def _():
                    arrive(gath.at[block_of(way, s), piece(i)], grecv.at[way, s - 1, i])

                @pl.when(s <= last - 1)
                def _():
                    forward(way, s, i)

    for i in range(2):
        for way in range(2):
            forward(way, 0, i)
    arrive(own.at[0], misc.at[0])
    for r in range(2):
        gath[z, 2 * (1 - c) + r] = own[c, 1 - c, r]
    for i in range(2, 4):
        for way in range(2):
            forward(way, 0, i)
    for d in range(1, n):
        send(gath.at[z], lraw.at[y], ssem.at[3], misc.at[2], dev(x, c, yp(d), z))
    for i in range(4):
        lraw[y, i] = gath[z, i]

    def combine(ref, parts, count):
        means = ref[0, 0:2, :]
        for q in range(1, parts):
            means += ref[q, 0:2, :]
        means = means / parts
        m1, m2 = means[0:1, :], means[1:2, :]
        s1 = s2 = s12 = jnp.zeros((1, LANE), f32)
        for q in range(parts):
            d1, d2 = ref[q, 0:1, :] - m1, ref[q, 1:2, :] - m2
            s1 += ref[q, 2:3, :] + count * (d1 * d1)
            s2 += ref[q, 3:4, :] + count * (d2 * d2)
            s12 += ref[q, 4:5, :] + count * (d1 * d2)
        return m1, m2, s1, s2, s12

    arrive(sty.at[pl.ds(0, n - 1)], misc.at[1])
    for r, v in enumerate(combine(sty, n, float(rows))):
        stz[z, r:r + 1, :] = v
    stz[z, 5:8, :] = jnp.zeros((3, LANE), f32)
    for d in far:
        send(stz.at[z], stz.at[z], ssem.at[4], misc.at[3], dev(x, c, y, zp(d)))
    for s in range(1, RING - 1):
        ring(s, range(4))
    arrive(stz.at[pl.ds(0, nz - 1)], misc.at[3])
    m1, m2, s1, s2, s12 = combine(stz, nz, float(group))
    i1 = lax.rsqrt(s1 / all_rows + epsilon)
    i2 = lax.rsqrt(s2 / all_rows + epsilon)
    mine = c * n + y
    for r, v in enumerate((m1, m2, i1, i2, s12 * i1 * i2 / all_rows)):
        mr[mine, r:r + 1, :] = v
    mr[mine, 5:8, :] = jnp.zeros((3, LANE), f32)
    for dc in range(2):
        for d in range(n):
            if d or dc:
                send(mr.at[mine], mr.at[mine], ssem.at[5], misc.at[4], dev(x, lax.rem(c + dc, 2), yp(d), z))
    ring(RING - 1, range(4))
    arrive(mr.at[pl.ds(0, 2 * n - 1)], misc.at[4])
    first = c == 0
    for q in range(2 * n):
        cols = slice(q * LANE, (q + 1) * LANE)
        for r, (u, v) in enumerate(((0, 1), (2, 3), (1, 0), (3, 2), (4, 4))):
            coef[r:r + 1, cols] = jnp.where(first, mr[q, u:u + 1, :], mr[q, v:v + 1, :])

    def standard(raw, h, r):
        cols = slice(h * COLS, (h + 1) * COLS)
        return (raw.astype(f32) - coef[r:r + 1, cols]) * coef[r + 1:r + 2, cols]

    arrive(lraw.at[pl.ds(0, n - 1)], misc.at[2])
    for q in range(n):
        for i in range(4):
            h, r = i // 2, i % 2
            nl[q * rows + r * hr:q * rows + (r + 1) * hr, h * COLS:(h + 1) * COLS] = standard(
                lraw[q, i], h, 0
            ).astype(bf16)

    def step(p, carry):
        ring(p + RING, range(2))

        @pl.when(p < half)
        def _():
            for k in range(2):
                block = zp(-p) if k == 0 else zp(p + 1)
                for i in range(4):
                    h, r = i // 2, i % 2
                    nr[p, k * rows + r * hr:k * rows + (r + 1) * hr, h * COLS:(h + 1) * COLS] = (
                        standard(gath[block, i], h, 0).astype(bf16)
                    )
            ksend[p] = lax.dot_general(
                nl[...], nr[p], (((1,), (1,)), ((), ())), preferred_element_type=f32
            ).astype(bf16).reshape(n, rows, 2 * rows)
            for d in range(1, n):
                send(ksend.at[p, xp(d)], arecv.at[p, d - 1], ssem.at[6], asem.at[p], dev(xp(d), c, y, z))

        ring(p + RING, range(2, 4))
        p1 = p - LAG

        @pl.when((p1 >= 0) & (p1 < half))
        def _():
            arrive(arecv.at[p1], asem.at[p1])
            s = ksend[p1, x].astype(f32)
            for d in range(n - 1):
                s += arecv[p1, d].astype(f32)
            dsend[p1] = s.astype(bf16)
            for d in range(n):
                send(dsend.at[p1], kfull.at[p1, x], ssem.at[7], dsem.at[p1], dev(xp(d), 1 - c, y, z))

        p2 = p - 2 * LAG

        @pl.when(p2 >= 0)
        def _():
            arrive(kfull.at[p2], dsem.at[p2])
            acc[...] += jnp.dot(
                kfull[p2].reshape(group, 2 * rows), nr[p2], preferred_element_type=f32
            ).reshape(n, rows, width)

        return carry

    lax.fori_loop(0, half + 2 * LAG, step, 0)

    plain = jnp.zeros((1, width), f32)
    times = jnp.zeros((1, width), f32)
    for q in range(n):
        v = acc[q]
        plain += jnp.sum(v, axis=0, keepdims=True)
        times += jnp.sum(v * nl[q * rows:(q + 1) * rows, :].astype(f32), axis=0, keepdims=True)
    tl[z, 0:1, :] = plain
    tl[z, 1:2, :] = times
    for d in far:
        send(tl.at[z], tl.at[z], ssem.at[8], misc.at[5], dev(x, c, y, zp(d)))
    for q in range(n):
        ysend[q] = acc[q].astype(bf16)
    for d in range(1, n):
        send(ysend.at[yp(d)], yrecv.at[d - 1], ssem.at[9], misc.at[6], dev(x, c, yp(d), z))
    arrive(tl.at[pl.ds(0, nz - 1)], misc.at[5])
    sums = tl[0]
    for q in range(1, nz):
        sums += tl[q]
    ty[y] = sums
    for d in range(1, n):
        send(ty.at[y], ty.at[y], ssem.at[10], misc.at[7], dev(x, c, yp(d), z))

    arrive(yrecv, misc.at[6])
    v = acc[y]
    for d in range(n - 1):
        v += yrecv[d].astype(f32)
    total[...] = v
    arrive(ty.at[pl.ds(0, n - 1)], misc.at[7])
    sums = ty[0]
    for q in range(1, n):
        sums += ty[q]
    sums = sums / all_rows
    diagonal = coef[4:5, :]
    scale = 2.0 * off_weight / all_rows
    lead = -2.0 * (1.0 - diagonal) - 2.0 * off_weight * diagonal

    terms = (1.0 - diagonal) * (1.0 - diagonal) + off_weight * (
        sums[1:2, :] / all_rows - diagonal * diagonal
    )
    lbx[t] = jnp.broadcast_to(
        jnp.sum(terms, axis=1, keepdims=True) * (0.5 / features), (1, LANE)
    )
    for dc in range(2):
        for d in range(n):
            if d or dc:
                send(lbx.at[t], lbx.at[t], ssem.at[11], misc.at[8], dev(xp(d), lax.rem(c + dc, 2), y, z))

    coef[5:6, :] = lead
    coef[6:7, :] = scale * sums[0:1, :]
    coef[7:8, :] = scale * sums[1:2, :] + lead * diagonal
    for h in range(2):
        cols = slice(h * COLS, (h + 1) * COLS)
        for r in range(2):
            lines = slice(r * hr, (r + 1) * hr)
            ours, theirs = standard(own[c, h, r], h, 0), standard(own[1 - c, h, r], h, 2)
            back = scale * total[lines, cols] + coef[5:6, cols] * theirs
            g = (back - coef[6:7, cols] - ours * coef[7:8, cols]) * coef[1:2, cols]
            gout[h, lines, :] = g.astype(bf16)
    send(gout.at[1 - c], outs.at[c], ssem.at[12], misc.at[9], dev(x, 1 - c, y, z))
    outs[c] = gout[c]
    arrive(outs.at[1 - c], misc.at[9])
    o1[...] = outs[0]
    o2[...] = outs[1]
    arrive(lbx.at[pl.ds(0, 2 * n - 1)], misc.at[8])
    part = lbx[0]
    for q in range(1, 2 * n):
        part += lbx[q]
    loss_ref[...] = part

    arrive(own.at[0], ssem.at[0])
    arrive(sty.at[pl.ds(0, n - 1)], ssem.at[1])
    arrive(gath.at[pl.ds(0, nz - 1)], ssem.at[2])
    arrive(lraw.at[pl.ds(0, n - 1)], ssem.at[3])
    arrive(stz.at[pl.ds(0, nz - 1)], ssem.at[4])
    arrive(mr.at[pl.ds(0, 2 * n - 1)], ssem.at[5])
    arrive(arecv, ssem.at[6])
    arrive(kfull, ssem.at[7])
    arrive(tl.at[pl.ds(0, nz - 1)], ssem.at[8])
    arrive(yrecv, ssem.at[9])
    arrive(ty.at[pl.ds(0, n - 1)], ssem.at[10])
    arrive(lbx.at[pl.ds(0, 2 * n - 1)], ssem.at[11])
    arrive(outs.at[0], ssem.at[12])


def local(first_view_output, second_view_output):
    n, nz, rows = SIDE, DEPTH, ROWS
    group, width, half = n * rows, 2 * COLS, nz // 2
    shape = first_view_output.shape
    vmem = pl.BlockSpec(memory_space=pltpu.VMEM)
    dma = pltpu.SemaphoreType.DMA
    g1, g2, loss = pl.pallas_call(
        kernel,
        out_shape=(
            jax.ShapeDtypeStruct(shape, bf16),
            jax.ShapeDtypeStruct(shape, bf16),
            jax.ShapeDtypeStruct((1, LANE), f32),
        ),
        in_specs=[vmem] * 2,
        out_specs=(vmem,) * 3,
        scratch_shapes=[
            pltpu.VMEM((2, 2, 2, rows // 2, COLS), bf16),
            pltpu.VMEM((nz, 4, rows // 2, COLS), bf16),
            pltpu.VMEM((n, 4, rows // 2, COLS), bf16),
            pltpu.VMEM((group, width), bf16),
            pltpu.VMEM((half, 2 * rows, width), bf16),
            pltpu.VMEM((n, 8, LANE), f32),
            pltpu.VMEM((n, 8, LANE), f32),
            pltpu.VMEM((nz, 8, LANE), f32),
            pltpu.VMEM((2 * n, 8, LANE), f32),
            pltpu.VMEM((8, width), f32),
            pltpu.VMEM((half, n, rows, 2 * rows), bf16),
            pltpu.VMEM((half, n - 1, rows, 2 * rows), bf16),
            pltpu.VMEM((half, rows, 2 * rows), bf16),
            pltpu.VMEM((half, n, rows, 2 * rows), bf16),
            pltpu.VMEM((n, rows, width), f32),
            pltpu.VMEM((nz, 2, width), f32),
            pltpu.VMEM((n, 2, width), f32),
            pltpu.VMEM((n, rows, width), bf16),
            pltpu.VMEM((n - 1, rows, width), bf16),
            pltpu.VMEM((rows, width), f32),
            pltpu.VMEM((2, rows, COLS), bf16),
            pltpu.VMEM((2, rows, COLS), bf16),
            pltpu.VMEM((2 * n, 1, LANE), f32),
            dma((13,)), dma((10,)), dma((2, half, 4)), dma((half,)), dma((half,)),
        ],
        compiler_params=pltpu.CompilerParams(
            collective_id=0, has_side_effects=True, vmem_limit_bytes=40 * 2**20
        ),
    )(first_view_output, second_view_output)
    return g1, g2, loss[0, 0]


def solution(mesh):
    spec = P("batch", "tile")
    return jax.shard_map(
        local, mesh=mesh, in_specs=(spec, spec), out_specs=(spec, spec, P()), check_vma=False
    )
```

time: 882 us -> 81.9 us (0.09)
  the two profiles are of different devices: /device:TPU:2 before, /device:TPU:1 now
where the time goes in v2:
time: 81.9 us; the launch traced here: 81.7 us
  Pallas kernels  76.9 us (94%)
  local copies, waits for them, and re-layouts  2.93 us (4%)
  between operations  1.81 us (2%)
    pallas_call x1, Pallas kernels, local(): pl.pallas_call(kernel, out_shape=(jax.ShapeDtypeStruct(shape, bf16), jax....  76.9 us
    unnamed x6, local copies, waits for them, and re-layouts  2.93 us

profile of v2, /device:TPU:1, one launch (start us, length us, event | category | flops | bytes accessed | tf_op | source)
XLA Modules:
  0.0 81.7 jit_solution(10695640432748832177)
XLA Ops:
  0.6 0.0 copy-start
  0.6 0.8 %copy-done = bf16[64,512]{1,0:T(8,128)(2,1)S(1)} copy-done((bf16[64,512]{1,0:T(8,128)(2,1)S(1)}, bf16[64,512]{1,0:T(8,128)(2,1)}, u32[]{:S(2)}) %copy-start) | copy-done | bytes 65560
  1.5 0.0 copy-start.1
  1.5 0.8 %copy-done.1 = bf16[64,512]{1,0:T(8,128)(2,1)S(1)} copy-done((bf16[64,512]{1,0:T(8,128)(2,1)S(1)}, bf16[64,512]{1,0:T(8,128)(2,1)}, u32[]{:S(2)}) %copy-start.1) | copy-done | bytes 65560
  2.3 76.9 %shard_map.49 = (bf16[64,512]{1,0:T(8,128)(2,1)S(1)}, bf16[64,512]{1,0:T(8,128)(2,1)S(1)}, f32[1,128]{1,0:T(1,128)S(1)}) custom-call(bf16[64,512]{1,0:T(8,128)(2,1)S(1)} %copy-done, bf16[64,512]{1,0:T(8,128)(2,1)S(1)} %copy-done.1), custom_call_target="tpu_custom_call" | custom-call | tf_op jit(solution)/shard_map/pallas_call | solution.py:328
  79.2 0.6 copy.8
  79.9 0.6 copy.9
Async XLA Ops:
  0.6 0.8 %copy-start = (bf16[64,512]{1,0:T(8,128)(2,1)S(1)}, bf16[64,512]{1,0:T(8,128)(2,1)}, u32[]{:S(2)}) copy-start(bf16[64,512]{1,0:T(8,128)(2,1)} %x1.1) | copy-start | bytes 196612
  1.5 0.8 %copy-start.1 = (bf16[64,512]{1,0:T(8,128)(2,1)S(1)}, bf16[64,512]{1,0:T(8,128)(2,1)}, u32[]{:S(2)}) copy-start(bf16[64,512]{1,0:T(8,128)(2,1)} %x2.1) | copy-start | bytes 196612

commit v3 on v2

v3 whole, which is shorter than its diff:
```python
import jax
import jax.numpy as jnp
from jax import lax
from jax.experimental import pallas as pl
from jax.experimental.pallas import tpu as pltpu
from jax.sharding import PartitionSpec as P

epsilon = 1e-05
off_weight = 0.0051
SIDE = 4
DEPTH = 16
ROWS = 64
COLS = 512
LANE = 128
PIECES = 4
LAG = 4
RING = 5
MESH = pl.DeviceIdType.MESH
f32, bf16 = jnp.float32, jnp.bfloat16


def kernel(
    x1, x2, o1, o2, loss_ref,
    own, gath, lraw, nl, nr, stl, sty, stz, mr, coef,
    ksend, arecv, dsend, kfull, acc, tl, tsend, ty, ysend, yrecv, params, lbx,
    ssem, misc, grecv, asem, dsem, lsem,
):
    n, nz, rows = SIDE, DEPTH, ROWS
    np = PIECES // 2
    hr = rows // np
    group = n * rows
    width = 2 * COLS
    half = nz // 2
    all_rows = float(group * nz)
    features = float(n * width)
    b, t = lax.axis_index("batch"), lax.axis_index("tile")
    y, z = b // nz, lax.rem(b, nz)
    x, c = t // 2, lax.rem(t, 2)

    def dev(x, c, y, z):
        return (y * nz + z, x * 2 + c)

    def xp(d):
        return lax.rem(x + d, n)

    def yp(d):
        return lax.rem(y + d, n)

    def zp(d):
        return lax.rem(z + d + nz, nz)

    def send(src, dst, out, into, to):
        pltpu.make_async_remote_copy(
            src_ref=src, dst_ref=dst, send_sem=out, recv_sem=into,
            device_id=to, device_id_type=MESH,
        ).start()

    def arrive(ref, sem):
        pltpu.make_async_copy(ref, ref, sem).wait()

    far = sorted(range(1, nz), key=lambda d: -min(d, nz - d))

    barrier = pltpu.get_barrier_semaphore()
    peers = 0
    for d in far:
        pl.semaphore_signal(barrier, 1, device_id=dev(x, c, y, zp(d)), device_id_type=MESH)
        peers += 1
    plane = [(dx, dc, dy) for dx in range(n) for dc in range(2) for dy in range(n)][1:]
    for dx, dc, dy in plane:
        to = dev(xp(dx), lax.rem(c + dc, 2), yp(dy), z)
        pl.semaphore_signal(barrier, 1, device_id=to, device_id_type=MESH)
        peers += 1
    loads = [pltpu.make_async_copy(ref, own.at[v, c], lsem.at[v]) for v, ref in enumerate((x1, x2))]
    for load in loads:
        load.start()
    acc[...] = jnp.zeros_like(acc)

    for load in loads:
        load.wait()
    for r in range(np):
        gath[z, np * c + r] = own[c, c, r * hr:(r + 1) * hr, :]
    for q in range(n):
        cols = slice(q * LANE, (q + 1) * LANE)
        v1 = own[0, c, :, cols].astype(f32)
        v2 = own[1, c, :, cols].astype(f32)
        a1 = jnp.sum(v1, axis=0, keepdims=True) / rows
        a2 = jnp.sum(v2, axis=0, keepdims=True) / rows
        v1, v2 = v1 - a1, v2 - a2
        stl[q, 0:1, :] = a1
        stl[q, 1:2, :] = a2
        stl[q, 2:3, :] = jnp.sum(v1 * v1, axis=0, keepdims=True)
        stl[q, 3:4, :] = jnp.sum(v2 * v2, axis=0, keepdims=True)
        stl[q, 4:5, :] = jnp.sum(v1 * v2, axis=0, keepdims=True)
    sty[y] = stl[y]
    pl.semaphore_wait(barrier, peers)

    send(own.at[1 - c, c], own.at[1 - c, c], ssem.at[0], misc.at[0], dev(x, 1 - c, y, z))
    for d in range(1, n):
        send(stl.at[yp(d)], sty.at[y], ssem.at[1], misc.at[1], dev(x, c, yp(d), z))

    def block_of(way, s):
        return zp(-s) if way == 0 else zp(s)

    def piece(i):
        return lax.rem(np * c + i, 2 * np)

    def forward(way, s, i):
        part = gath.at[block_of(way, s), piece(i)]
        to = zp(1) if way == 0 else zp(-1)
        send(part, part, ssem.at[2], grecv.at[way, s, i], dev(x, c, y, to))

    def ring(u):
        s, g = u // 2, u % 2
        for k in range(np):
            i = np * g + k
            for way in range(2):
                last = half - g if way == 0 else half - 1 + g

                @pl.when(s <= last)
                def _():
                    arrive(gath.at[block_of(way, s), piece(i)], grecv.at[way, s - 1, i])

                @pl.when(s <= last - 1)
                def _():
                    forward(way, s, i)

    for i in range(np):
        for way in range(2):
            forward(way, 0, i)
    arrive(own.at[0, 0], misc.at[0])
    for r in range(np):
        gath[z, np * (1 - c) + r] = own[c, 1 - c, r * hr:(r + 1) * hr, :]
    for i in range(np, 2 * np):
        for way in range(2):
            forward(way, 0, i)
    for d in range(1, n):
        send(gath.at[z], lraw.at[y], ssem.at[3], misc.at[2], dev(x, c, yp(d), z))
    for i in range(2 * np):
        lraw[y, i] = gath[z, i]

    def combine(ref, parts, count):
        means = ref[0, 0:2, :]
        for q in range(1, parts):
            means += ref[q, 0:2, :]
        means = means / parts
        m1, m2 = means[0:1, :], means[1:2, :]
        s1 = s2 = s12 = jnp.zeros((1, LANE), f32)
        for q in range(parts):
            d1, d2 = ref[q, 0:1, :] - m1, ref[q, 1:2, :] - m2
            s1 += ref[q, 2:3, :] + count * (d1 * d1)
            s2 += ref[q, 3:4, :] + count * (d2 * d2)
            s12 += ref[q, 4:5, :] + count * (d1 * d2)
        return m1, m2, s1, s2, s12

    ring(2)
    arrive(sty.at[pl.ds(0, n - 1)], misc.at[1])
    for r, v in enumerate(combine(sty, n, float(rows))):
        stz[z, r:r + 1, :] = v
    for d in far:
        send(stz.at[z], stz.at[z], ssem.at[4], misc.at[3], dev(x, c, y, zp(d)))
    for u in range(3, 2 * RING - 2):
        ring(u)
    arrive(stz.at[pl.ds(0, nz - 1)], misc.at[3])
    m1, m2, s1, s2, s12 = combine(stz, nz, float(group))
    i1 = lax.rsqrt(s1 / all_rows + epsilon)
    i2 = lax.rsqrt(s2 / all_rows + epsilon)
    mine = c * n + y
    for r, v in enumerate((m1, m2, i1, i2, s12 * i1 * i2 / all_rows)):
        mr[mine, r:r + 1, :] = v
    for dc in range(2):
        for d in range(n):
            if d or dc:
                send(mr.at[mine], mr.at[mine], ssem.at[5], misc.at[4], dev(x, lax.rem(c + dc, 2), yp(d), z))
    ring(2 * RING - 2)
    ring(2 * RING - 1)
    arrive(mr.at[pl.ds(0, 2 * n - 1)], misc.at[4])
    first = c == 0
    for q in range(2 * n):
        cols = slice(q * LANE, (q + 1) * LANE)
        for r, (u, v) in enumerate(((0, 1), (2, 3), (4, 4))):
            coef[r:r + 1, cols] = jnp.where(first, mr[q, u:u + 1, :], mr[q, v:v + 1, :])

    def standard(raw, h):
        cols = slice(h * COLS, (h + 1) * COLS)
        return (raw.astype(f32) - coef[0:1, cols]) * coef[1:2, cols]

    arrive(lraw.at[pl.ds(0, n - 1)], misc.at[2])
    for q in range(n):
        for i in range(2 * np):
            h, r = i // np, i % np
            nl[q * rows + r * hr:q * rows + (r + 1) * hr, h * COLS:(h + 1) * COLS] = standard(
                lraw[q, i], h
            ).astype(bf16)

    def step(p, carry):
        ring(p + 2 * RING)

        @pl.when(p < half)
        def _():
            for k in range(2):
                block = zp(-p) if k == 0 else zp(p + 1)
                for i in range(2 * np):
                    h, r = i // np, i % np
                    nr[
                        p // 2,
                        pl.ds(pl.multiple_of(lax.rem(p, 2) * 2 * rows + k * rows + r * hr, hr), hr),
                        h * COLS:(h + 1) * COLS,
                    ] = (
                        standard(gath[block, i], h).astype(bf16)
                    )
            ksend[p] = lax.dot_general(
                nl[...], nr[p // 2, pl.ds(pl.multiple_of(lax.rem(p, 2) * 2 * rows, 2 * rows), 2 * rows), :],
                (((1,), (1,)), ((), ())), preferred_element_type=f32,
            ).astype(bf16).reshape(n, rows, 2 * rows)
            for d in range(1, n):
                send(ksend.at[p, xp(d)], arecv.at[p, d - 1], ssem.at[6], asem.at[p], dev(xp(d), c, y, z))

        p1 = p - LAG

        @pl.when((p1 >= 0) & (p1 < half))
        def _():
            arrive(arecv.at[p1], asem.at[p1])
            s = ksend[p1, x].astype(f32)
            for d in range(n - 1):
                s += arecv[p1, d].astype(f32)
            dsend[p1] = s.astype(bf16)
            for d in range(n):
                send(
                    dsend.at[p1],
                    kfull.at[p1 // 2, x, :, pl.ds(pl.multiple_of(lax.rem(p1, 2) * 2 * rows, 2 * rows), 2 * rows)],
                    ssem.at[7], dsem.at[p1 // 2], dev(xp(d), 1 - c, y, z),
                )

        p2 = p - 2 * LAG

        @pl.when((p2 >= 0) & (lax.rem(p2, 2) == 1))
        def _():
            two = p2 // 2
            arrive(kfull.at[two], dsem.at[two])
            acc[...] += jnp.dot(
                kfull[two].reshape(group, 4 * rows), nr[two], preferred_element_type=f32
            ).reshape(n, rows, width)

        return carry

    lax.fori_loop(0, half + 2 * LAG, step, 0)

    plain = jnp.zeros((1, width), f32)
    times = jnp.zeros((1, width), f32)
    for q in range(n):
        v = acc[q]
        plain += jnp.sum(v, axis=0, keepdims=True)
        times += jnp.sum(v * nl[q * rows:(q + 1) * rows, :].astype(f32), axis=0, keepdims=True)
    tl[z, 0:1, :] = plain
    tl[z, 1:2, :] = times
    for d in far:
        send(tl.at[z], tl.at[z], ssem.at[8], misc.at[5], dev(x, c, y, zp(d)))
    for q in range(n):
        for h in range(2):
            ysend[q, h] = acc[q, :, h * COLS:(h + 1) * COLS].astype(bf16)
    row = [(dc, d) for dc in range(2) for d in range(n)][1:]
    for dc, d in row:
        cc, yy = lax.rem(c + dc, 2), yp(d)
        send(ysend.at[yy, cc], yrecv.at[c * n + y], ssem.at[9], misc.at[6], dev(x, cc, yy, z))
    yrecv[c * n + y] = ysend[y, c]
    arrive(tl.at[pl.ds(0, nz - 1)], misc.at[5])
    sums = tl[0]
    for q in range(1, nz):
        sums += tl[q]
    for h in range(2):
        tsend[h] = sums[:, h * COLS:(h + 1) * COLS]
    for dc, d in row:
        cc, yy = lax.rem(c + dc, 2), yp(d)
        send(tsend.at[cc], ty.at[c * n + y], ssem.at[10], misc.at[7], dev(x, cc, yy, z))
    ty[c * n + y] = tsend[c]
    diagonal = coef[2:3, :]
    terms = ((1.0 - diagonal) * (1.0 - diagonal) - off_weight * diagonal * diagonal) / n + (
        off_weight / (all_rows * all_rows)
    ) * sums[1:2, :]
    place = t * n + y
    lbx[place] = jnp.broadcast_to(
        jnp.sum(terms, axis=1, keepdims=True) * (0.5 / features), (1, LANE)
    )
    for dx, dc, dy in plane:
        to = dev(xp(dx), lax.rem(c + dc, 2), yp(dy), z)
        send(lbx.at[place], lbx.at[place], ssem.at[11], misc.at[8], to)

    scale = 2.0 * off_weight / all_rows
    for q in range(n):
        cols = slice(q * LANE, (q + 1) * LANE)
        for r in range(5):
            params[r:r + 1, cols] = mr[c * n + q, r:r + 1, :]
    diagonal = params[4:5, :]
    lead = -2.0 * (1.0 - diagonal) - 2.0 * off_weight * diagonal
    hats = [
        (own[v, c].astype(f32) - params[v:v + 1, :]) * params[2 + v:3 + v, :] for v in range(2)
    ]
    arrive(yrecv.at[pl.ds(0, 2 * n - 1)], misc.at[6])
    arrive(ty.at[pl.ds(0, 2 * n - 1)], misc.at[7])
    for v, out in enumerate((o1, o2)):
        product = yrecv[v * n].astype(f32)
        sums = ty[v * n]
        for q in range(1, n):
            product += yrecv[v * n + q].astype(f32)
            sums += ty[v * n + q]
        sums = sums * (scale / all_rows)
        back = scale * product + lead * hats[1 - v]
        g = back - sums[0:1, :] - hats[v] * (sums[1:2, :] + lead * diagonal)
        out[...] = (g * params[2 + v:3 + v, :]).astype(bf16)
    arrive(lbx.at[pl.ds(0, 2 * n * n - 1)], misc.at[8])
    part = lbx[0]
    for q in range(1, 2 * n * n):
        part += lbx[q]
    loss_ref[...] = part

    arrive(own.at[0, 0], ssem.at[0])
    arrive(sty.at[pl.ds(0, n - 1)], ssem.at[1])
    arrive(gath.at[pl.ds(0, nz - 1)], ssem.at[2])
    arrive(lraw.at[pl.ds(0, n - 1)], ssem.at[3])
    arrive(stz.at[pl.ds(0, nz - 1)], ssem.at[4])
    arrive(mr.at[pl.ds(0, 2 * n - 1)], ssem.at[5])
    arrive(arecv, ssem.at[6])
    arrive(kfull, ssem.at[7])
    arrive(tl.at[pl.ds(0, nz - 1)], ssem.at[8])
    arrive(yrecv.at[pl.ds(0, 2 * n - 1)], ssem.at[9])
    arrive(ty.at[pl.ds(0, 2 * n - 1)], ssem.at[10])
    arrive(lbx.at[pl.ds(0, 2 * n * n - 1)], ssem.at[11])


def local(first_view_output, second_view_output):
    n, nz, rows = SIDE, DEPTH, ROWS
    group, width, half, np = n * rows, 2 * COLS, nz // 2, PIECES // 2
    shape = first_view_output.shape
    vmem = pl.BlockSpec(memory_space=pltpu.VMEM)
    dma = pltpu.SemaphoreType.DMA
    g1, g2, loss = pl.pallas_call(
        kernel,
        out_shape=(
            jax.ShapeDtypeStruct(shape, bf16),
            jax.ShapeDtypeStruct(shape, bf16),
            jax.ShapeDtypeStruct((1, LANE), f32),
        ),
        in_specs=[pl.BlockSpec(memory_space=pl.ANY)] * 2,
        out_specs=(vmem,) * 3,
        scratch_shapes=[
            pltpu.VMEM((2, 2, rows, COLS), bf16),
            pltpu.VMEM((nz, 2 * np, rows // np, COLS), bf16),
            pltpu.VMEM((n, 2 * np, rows // np, COLS), bf16),
            pltpu.VMEM((group, width), bf16),
            pltpu.VMEM((half // 2, 4 * rows, width), bf16),
            pltpu.VMEM((n, 5, LANE), f32),
            pltpu.VMEM((n, 5, LANE), f32),
            pltpu.VMEM((nz, 5, LANE), f32),
            pltpu.VMEM((2 * n, 5, LANE), f32),
            pltpu.VMEM((8, width), f32),
            pltpu.VMEM((half, n, rows, 2 * rows), bf16),
            pltpu.VMEM((half, n - 1, rows, 2 * rows), bf16),
            pltpu.VMEM((half, rows, 2 * rows), bf16),
            pltpu.VMEM((half // 2, n, rows, 4 * rows), bf16),
            pltpu.VMEM((n, rows, width), f32),
            pltpu.VMEM((nz, 2, width), f32),
            pltpu.VMEM((2, 2, COLS), f32),
            pltpu.VMEM((2 * n, 2, COLS), f32),
            pltpu.VMEM((n, 2, rows, COLS), bf16),
            pltpu.VMEM((2 * n, rows, COLS), bf16),
            pltpu.VMEM((8, COLS), f32),
            pltpu.VMEM((2 * n * n, 1, LANE), f32),
            dma((12,)), dma((9,)), dma((2, half, PIECES)), dma((half,)), dma((half,)), dma((2,)),
        ],
        compiler_params=pltpu.CompilerParams(
            collective_id=0, has_side_effects=True, vmem_limit_bytes=40 * 2**20
        ),
    )(first_view_output, second_view_output)
    return g1, g2, loss[0, 0]


def solution(mesh):
    spec = P("batch", "tile")
    return jax.shard_map(
        local, mesh=mesh, in_specs=(spec, spec), out_specs=(spec, spec, P()), check_vma=False
    )
```

time: 81.9 us -> 74.1 us (0.905)
  Pallas kernels: 76.9 us -> 69.1 us
    pallas_call x1, Pallas kernels: 76.9 us -> 69.1 us  [local(): pl.pallas_call(kernel, out_shape=(jax.ShapeDtypeStruct(shape, bf16), jax....]
where the time goes in v3:
time: 74.1 us; the launch traced here: 73.9 us
  Pallas kernels  69.1 us (93%)
  local copies, waits for them, and re-layouts  2.93 us (4%)
  between operations  1.81 us (2%)
    pallas_call x1, Pallas kernels, local(): pl.pallas_call(kernel, out_shape=(jax.ShapeDtypeStruct(shape, bf16), jax....  69.1 us
    unnamed x6, local copies, waits for them, and re-layouts  2.93 us

profile of v3, /device:TPU:1, one launch (start us, length us, event | category | flops | bytes accessed | tf_op | source)
XLA Modules:
  0.0 73.9 jit_solution(9150969848021016203)
XLA Ops:
  0.6 0.0 copy-start
  0.6 0.8 %copy-done = bf16[64,512]{1,0:T(8,128)(2,1)S(1)} copy-done((bf16[64,512]{1,0:T(8,128)(2,1)S(1)}, bf16[64,512]{1,0:T(8,128)(2,1)}, u32[]{:S(2)}) %copy-start) | copy-done | bytes 65560
  1.5 0.0 copy-start.1
  1.5 0.8 %copy-done.1 = bf16[64,512]{1,0:T(8,128)(2,1)S(1)} copy-done((bf16[64,512]{1,0:T(8,128)(2,1)S(1)}, bf16[64,512]{1,0:T(8,128)(2,1)}, u32[]{:S(2)}) %copy-start.1) | copy-done | bytes 65560
  2.3 69.1 %shard_map.49 = (bf16[64,512]{1,0:T(8,128)(2,1)S(1)}, bf16[64,512]{1,0:T(8,128)(2,1)S(1)}, f32[1,128]{1,0:T(1,128)S(1)}) custom-call(bf16[64,512]{1,0:T(8,128)(2,1)S(1)} %copy-done, bf16[64,512]{1,0:T(8,128)(2,1)S(1)} %copy-done.1), custom_call_target="tpu_custom_call" | custom-call | tf_op jit(solution)/shard_map/pallas_call | solution.py:336
  71.4 0.6 copy.8
  72.1 0.6 copy.9
Async XLA Ops:
  0.6 0.8 %copy-start = (bf16[64,512]{1,0:T(8,128)(2,1)S(1)}, bf16[64,512]{1,0:T(8,128)(2,1)}, u32[]{:S(2)}) copy-start(bf16[64,512]{1,0:T(8,128)(2,1)} %x1.1) | copy-start | bytes 196612
  1.5 0.8 %copy-start.1 = (bf16[64,512]{1,0:T(8,128)(2,1)S(1)}, bf16[64,512]{1,0:T(8,128)(2,1)}, u32[]{:S(2)}) copy-start(bf16[64,512]{1,0:T(8,128)(2,1)} %x2.1) | copy-start | bytes 196612

commit v4 on v3

--- a/solution.py
+++ b/solution.py
@@ -13,8 +13,7 @@
 COLS = 512
 LANE = 128
 PIECES = 4
-LAG = 4
-RING = 5
+RING = 4
 MESH = pl.DeviceIdType.MESH
 f32, bf16 = jnp.float32, jnp.bfloat16
 
@@ -22,8 +21,8 @@
 def kernel(
     x1, x2, o1, o2, loss_ref,
     own, gath, lraw, nl, nr, stl, sty, stz, mr, coef,
-    ksend, arecv, dsend, kfull, acc, tl, tsend, ty, ysend, yrecv, params, lbx,
-    ssem, misc, grecv, asem, dsem, lsem,
+    ksend, arecv, dsend, kfull, klast, acc, tl, tsend, ty, ysend, yrecv, params, lbx,
+    ssem, misc, grecv, asem, dsem, lsem, lastsem,
 ):
     n, nz, rows = SIDE, DEPTH, ROWS
     np = PIECES // 2
@@ -94,10 +93,6 @@
     sty[y] = stl[y]
     pl.semaphore_wait(barrier, peers)
 
-    send(own.at[1 - c, c], own.at[1 - c, c], ssem.at[0], misc.at[0], dev(x, 1 - c, y, z))
-    for d in range(1, n):
-        send(stl.at[yp(d)], sty.at[y], ssem.at[1], misc.at[1], dev(x, c, yp(d), z))
-
     def block_of(way, s):
         return zp(-s) if way == 0 else zp(s)
 
@@ -124,9 +119,12 @@
                 def _():
                     forward(way, s, i)
 
+    send(own.at[1 - c, c], own.at[1 - c, c], ssem.at[0], misc.at[0], dev(x, 1 - c, y, z))
     for i in range(np):
         for way in range(2):
             forward(way, 0, i)
+    for d in range(1, n):
+        send(stl.at[yp(d)], sty.at[y], ssem.at[1], misc.at[1], dev(x, c, yp(d), z))
     arrive(own.at[0, 0], misc.at[0])
     for r in range(np):
         gath[z, np * (1 - c) + r] = own[c, 1 - c, r * hr:(r + 1) * hr, :]
@@ -192,58 +190,69 @@
                 lraw[q, i], h
             ).astype(bf16)
 
-    def step(p, carry):
-        ring(p + 2 * RING)
-
-        @pl.when(p < half)
-        def _():
-            for k in range(2):
-                block = zp(-p) if k == 0 else zp(p + 1)
-                for i in range(2 * np):
-                    h, r = i // np, i % np
-                    nr[
-                        p // 2,
-                        pl.ds(pl.multiple_of(lax.rem(p, 2) * 2 * rows + k * rows + r * hr, hr), hr),
-                        h * COLS:(h + 1) * COLS,
-                    ] = (
-                        standard(gath[block, i], h).astype(bf16)
-                    )
-            ksend[p] = lax.dot_general(
-                nl[...], nr[p // 2, pl.ds(pl.multiple_of(lax.rem(p, 2) * 2 * rows, 2 * rows), 2 * rows), :],
-                (((1,), (1,)), ((), ())), preferred_element_type=f32,
-            ).astype(bf16).reshape(n, rows, 2 * rows)
+    def multiply(p):
+        place = pl.ds((p % 2) * 2 * rows, 2 * rows)
+        for k in range(2):
+            block = zp(-p) if k == 0 else zp(p + 1)
+            for i in range(2 * np):
+                h, r = i // np, i % np
+                start = (p % 2) * 2 * rows + k * rows + r * hr
+                nr[p // 2, start:start + hr, h * COLS:(h + 1) * COLS] = standard(
+                    gath[block, i], h
+                ).astype(bf16)
+        ksend[p] = lax.dot_general(
+            nl[...], nr[p // 2, place, :], (((1,), (1,)), ((), ())), preferred_element_type=f32
+        ).astype(bf16).reshape(n, rows, 2 * rows)
+        if p == half - 1:
+            for d in range(n):
+                send(ksend.at[p], klast.at[x], ssem.at[8], lastsem, dev(xp(d), 1 - c, y, z))
+            return
+        for d in range(1, n):
+            send(ksend.at[p, xp(d)], arecv.at[p, d - 1], ssem.at[6], asem.at[p], dev(xp(d), c, y, z))
+
+    def reduce(p):
+        place = pl.ds((p % 2) * 2 * rows, 2 * rows)
+        arrive(arecv.at[p], asem.at[p])
+        s = ksend[p, x].astype(f32)
+        for d in range(n - 1):
+            s += arecv[p, d].astype(f32)
+        dsend[p] = s.astype(bf16)
+        for d in range(n):
+            send(
+                dsend.at[p], kfull.at[p // 2, x, :, place], ssem.at[7], dsem.at[p // 2],
+                dev(xp(d), 1 - c, y, z),
+            )
+
+    def consume(two):
+        arrive(kfull.at[two], dsem.at[two])
+        acc[...] += jnp.dot(
+            kfull[two].reshape(group, 4 * rows), nr[two], preferred_element_type=f32
+        ).reshape(n, rows, width)
+
+    def finish(p):
+        k = p % 2
+        if k == 0:
+            arrive(kfull.at[p // 2, :, :, pl.ds(0, 2 * rows)], dsem.at[p // 2])
+            s = kfull[p // 2, :, :, 0:2 * rows]
+        else:
+            arrive(klast, lastsem)
+            s = klast[0].astype(f32)
             for d in range(1, n):
-                send(ksend.at[p, xp(d)], arecv.at[p, d - 1], ssem.at[6], asem.at[p], dev(xp(d), c, y, z))
-
-        p1 = p - LAG
-
-        @pl.when((p1 >= 0) & (p1 < half))
-        def _():
-            arrive(arecv.at[p1], asem.at[p1])
-            s = ksend[p1, x].astype(f32)
-            for d in range(n - 1):
-                s += arecv[p1, d].astype(f32)
-            dsend[p1] = s.astype(bf16)
-            for d in range(n):
-                send(
-                    dsend.at[p1],
-                    kfull.at[p1 // 2, x, :, pl.ds(pl.multiple_of(lax.rem(p1, 2) * 2 * rows, 2 * rows), 2 * rows)],
-                    ssem.at[7], dsem.at[p1 // 2], dev(xp(d), 1 - c, y, z),
-                )
-
-        p2 = p - 2 * LAG
-
-        @pl.when((p2 >= 0) & (lax.rem(p2, 2) == 1))
-        def _():
-            two = p2 // 2
-            arrive(kfull.at[two], dsem.at[two])
-            acc[...] += jnp.dot(
-                kfull[two].reshape(group, 4 * rows), nr[two], preferred_element_type=f32
-            ).reshape(n, rows, width)
-
-        return carry
-
-    lax.fori_loop(0, half + 2 * LAG, step, 0)
+                s += klast[d].astype(f32)
+            s = s.astype(bf16)
+        acc[...] += jnp.dot(
+            s.reshape(group, 2 * rows), nr[p // 2, k * 2 * rows:(k + 1) * 2 * rows, :],
+            preferred_element_type=f32,
+        ).reshape(n, rows, width)
+
+    for work, p in (
+        (ring, 8), (multiply, 0), (ring, 9), (multiply, 1), (ring, 10), (multiply, 2),
+        (ring, 11), (multiply, 3), (reduce, 0), (ring, 12), (reduce, 1), (ring, 13),
+        (multiply, 4), (multiply, 5), (ring, 14), (reduce, 2), (reduce, 3), (ring, 15),
+        (multiply, 6), (consume, 0), (reduce, 4), (ring, 16), (ring, 17), (multiply, 7),
+        (reduce, 5), (reduce, 6), (consume, 1), (consume, 2), (finish, 6), (finish, 7),
+    ):
+        work(p)
 
     plain = jnp.zeros((1, width), f32)
     times = jnp.zeros((1, width), f32)
@@ -254,14 +263,14 @@
     tl[z, 0:1, :] = plain
     tl[z, 1:2, :] = times
     for d in far:
-        send(tl.at[z], tl.at[z], ssem.at[8], misc.at[5], dev(x, c, y, zp(d)))
+        send(tl.at[z], tl.at[z], ssem.at[9], misc.at[5], dev(x, c, y, zp(d)))
     for q in range(n):
         for h in range(2):
             ysend[q, h] = acc[q, :, h * COLS:(h + 1) * COLS].astype(bf16)
     row = [(dc, d) for dc in range(2) for d in range(n)][1:]
     for dc, d in row:
         cc, yy = lax.rem(c + dc, 2), yp(d)
-        send(ysend.at[yy, cc], yrecv.at[c * n + y], ssem.at[9], misc.at[6], dev(x, cc, yy, z))
+        send(ysend.at[yy, cc], yrecv.at[c * n + y], ssem.at[10], misc.at[6], dev(x, cc, yy, z))
     yrecv[c * n + y] = ysend[y, c]
     arrive(tl.at[pl.ds(0, nz - 1)], misc.at[5])
     sums = tl[0]
@@ -271,7 +280,7 @@
         tsend[h] = sums[:, h * COLS:(h + 1) * COLS]
     for dc, d in row:
         cc, yy = lax.rem(c + dc, 2), yp(d)
-        send(tsend.at[cc], ty.at[c * n + y], ssem.at[10], misc.at[7], dev(x, cc, yy, z))
+        send(tsend.at[cc], ty.at[c * n + y], ssem.at[11], misc.at[7], dev(x, cc, yy, z))
     ty[c * n + y] = tsend[c]
     diagonal = coef[2:3, :]
     terms = ((1.0 - diagonal) * (1.0 - diagonal) - off_weight * diagonal * diagonal) / n + (
@@ -283,7 +292,7 @@
     )
     for dx, dc, dy in plane:
         to = dev(xp(dx), lax.rem(c + dc, 2), yp(dy), z)
-        send(lbx.at[place], lbx.at[place], ssem.at[11], misc.at[8], to)
+        send(lbx.at[place], lbx.at[place], ssem.at[12], misc.at[8], to)
 
     scale = 2.0 * off_weight / all_rows
     for q in range(n):
@@ -319,12 +328,13 @@
     arrive(lraw.at[pl.ds(0, n - 1)], ssem.at[3])
     arrive(stz.at[pl.ds(0, nz - 1)], ssem.at[4])
     arrive(mr.at[pl.ds(0, 2 * n - 1)], ssem.at[5])
-    arrive(arecv, ssem.at[6])
-    arrive(kfull, ssem.at[7])
-    arrive(tl.at[pl.ds(0, nz - 1)], ssem.at[8])
-    arrive(yrecv.at[pl.ds(0, 2 * n - 1)], ssem.at[9])
-    arrive(ty.at[pl.ds(0, 2 * n - 1)], ssem.at[10])
-    arrive(lbx.at[pl.ds(0, 2 * n * n - 1)], ssem.at[11])
+    arrive(arecv.at[pl.ds(0, half - 1)], ssem.at[6])
+    arrive(ksend.at[pl.ds(0, half - 1)], ssem.at[7])
+    arrive(klast, ssem.at[8])
+    arrive(tl.at[pl.ds(0, nz - 1)], ssem.at[9])
+    arrive(yrecv.at[pl.ds(0, 2 * n - 1)], ssem.at[10])
+    arrive(ty.at[pl.ds(0, 2 * n - 1)], ssem.at[11])
+    arrive(lbx.at[pl.ds(0, 2 * n * n - 1)], ssem.at[12])
 
 
 def local(first_view_output, second_view_output):
@@ -340,7 +350,7 @@
             jax.ShapeDtypeStruct(shape, bf16),
             jax.ShapeDtypeStruct((1, LANE), f32),
         ),
-        in_specs=[pl.BlockSpec(memory_space=pl.ANY)] * 2,
+        in_specs=[pl.BlockSpec(memory_space=pltpu.HBM)] * 2,
         out_specs=(vmem,) * 3,
         scratch_shapes=[
             pltpu.VMEM((2, 2, rows, COLS), bf16),
@@ -357,6 +367,7 @@
             pltpu.VMEM((half, n - 1, rows, 2 * rows), bf16),
             pltpu.VMEM((half, rows, 2 * rows), bf16),
             pltpu.VMEM((half // 2, n, rows, 4 * rows), bf16),
+            pltpu.VMEM((n, n, rows, 2 * rows), bf16),
             pltpu.VMEM((n, rows, width), f32),
             pltpu.VMEM((nz, 2, width), f32),
             pltpu.VMEM((2, 2, COLS), f32),
@@ -365,7 +376,7 @@
             pltpu.VMEM((2 * n, rows, COLS), bf16),
             pltpu.VMEM((8, COLS), f32),
             pltpu.VMEM((2 * n * n, 1, LANE), f32),
-            dma((12,)), dma((9,)), dma((2, half, PIECES)), dma((half,)), dma((half,)), dma((2,)),
+            dma((13,)), dma((9,)), dma((2, half, PIECES)), dma((half,)), dma((half,)), dma((2,)), dma,
         ],
         compiler_params=pltpu.CompilerParams(
             collective_id=0, has_side_effects=True, vmem_limit_bytes=40 * 2**20

time: 74.1 us -> 72.2 us (0.974)
  Pallas kernels: 69.1 us -> 67.2 us
    pallas_call x1, Pallas kernels: 69.1 us -> 67.2 us  [local(): pl.pallas_call(kernel, out_shape=(jax.ShapeDtypeStruct(shape, bf16), jax....]
where the time goes in v4:
time: 72.2 us; the launch traced here: 71.9 us
  Pallas kernels  67.2 us (93%)
  local copies, waits for them, and re-layouts  2.93 us (4%)
  between operations  1.81 us (3%)
    pallas_call x1, Pallas kernels, local(): pl.pallas_call(kernel, out_shape=(jax.ShapeDtypeStruct(shape, bf16), jax....  67.2 us
    unnamed x6, local copies, waits for them, and re-layouts  2.93 us

profile of v4, /device:TPU:1, one launch (start us, length us, event | category | flops | bytes accessed | tf_op | source)
XLA Modules:
  0.0 71.9 jit_solution(1082861807180210425)
XLA Ops:
  0.6 0.0 copy-start
  0.6 0.8 %copy-done = bf16[64,512]{1,0:T(8,128)(2,1)S(1)} copy-done((bf16[64,512]{1,0:T(8,128)(2,1)S(1)}, bf16[64,512]{1,0:T(8,128)(2,1)}, u32[]{:S(2)}) %copy-start) | copy-done | bytes 65560
  1.5 0.0 copy-start.1
  1.5 0.8 %copy-done.1 = bf16[64,512]{1,0:T(8,128)(2,1)S(1)} copy-done((bf16[64,512]{1,0:T(8,128)(2,1)S(1)}, bf16[64,512]{1,0:T(8,128)(2,1)}, u32[]{:S(2)}) %copy-start.1) | copy-done | bytes 65560
  2.3 67.2 %shard_map.49 = (bf16[64,512]{1,0:T(8,128)(2,1)S(1)}, bf16[64,512]{1,0:T(8,128)(2,1)S(1)}, f32[1,128]{1,0:T(1,128)S(1)}) custom-call(bf16[64,512]{1,0:T(8,128)(2,1)S(1)} %copy-done, bf16[64,512]{1,0:T(8,128)(2,1)S(1)} %copy-done.1), custom_call_target="tpu_custom_call" | custom-call | tf_op jit(solution)/shard_map/pallas_call | solution.py:346
  69.5 0.6 copy.8
  70.1 0.6 copy.9
Async XLA Ops:
  0.6 0.8 %copy-start = (bf16[64,512]{1,0:T(8,128)(2,1)S(1)}, bf16[64,512]{1,0:T(8,128)(2,1)}, u32[]{:S(2)}) copy-start(bf16[64,512]{1,0:T(8,128)(2,1)} %x1.1) | copy-start | bytes 196612
  1.5 0.8 %copy-start.1 = (bf16[64,512]{1,0:T(8,128)(2,1)S(1)}, bf16[64,512]{1,0:T(8,128)(2,1)}, u32[]{:S(2)}) copy-start(bf16[64,512]{1,0:T(8,128)(2,1)} %x2.1) | copy-start | bytes 196612

commit v5 on v4

--- a/solution.py
+++ b/solution.py
@@ -21,7 +21,7 @@
 def kernel(
     x1, x2, o1, o2, loss_ref,
     own, gath, lraw, nl, nr, stl, sty, stz, mr, coef,
-    ksend, arecv, dsend, kfull, klast, acc, tl, tsend, ty, ysend, yrecv, params, lbx,
+    ksend, arecv, dsend, kfull, klast, kall, acc, tl, tsend, ty, ysend, yrecv, params, lbx,
     ssem, misc, grecv, asem, dsem, lsem, lastsem,
 ):
     n, nz, rows = SIDE, DEPTH, ROWS
@@ -150,13 +150,12 @@
             s12 += ref[q, 4:5, :] + count * (d1 * d2)
         return m1, m2, s1, s2, s12
 
-    ring(2)
     arrive(sty.at[pl.ds(0, n - 1)], misc.at[1])
     for r, v in enumerate(combine(sty, n, float(rows))):
         stz[z, r:r + 1, :] = v
     for d in far:
         send(stz.at[z], stz.at[z], ssem.at[4], misc.at[3], dev(x, c, y, zp(d)))
-    for u in range(3, 2 * RING - 2):
+    for u in range(2, 2 * RING - 2):
         ring(u)
     arrive(stz.at[pl.ds(0, nz - 1)], misc.at[3])
     m1, m2, s1, s2, s12 = combine(stz, nz, float(group))
@@ -190,25 +189,32 @@
                 lraw[q, i], h
             ).astype(bf16)
 
+    def normalize(block, to, start):
+        for i in range(2 * np):
+            h, r = i // np, i % np
+            lines = slice(start + r * hr, start + (r + 1) * hr)
+            nr[to, lines, h * COLS:(h + 1) * COLS] = standard(gath[block, i], h).astype(bf16)
+
     def multiply(p):
-        place = pl.ds((p % 2) * 2 * rows, 2 * rows)
-        for k in range(2):
-            block = zp(-p) if k == 0 else zp(p + 1)
-            for i in range(2 * np):
-                h, r = i // np, i % np
-                start = (p % 2) * 2 * rows + k * rows + r * hr
-                nr[p // 2, start:start + hr, h * COLS:(h + 1) * COLS] = standard(
-                    gath[block, i], h
-                ).astype(bf16)
+        start = (p % 2) * 2 * rows
+        normalize(zp(-p), p // 2, start)
+        normalize(zp(p + 1), p // 2, start + rows)
         ksend[p] = lax.dot_general(
-            nl[...], nr[p // 2, place, :], (((1,), (1,)), ((), ())), preferred_element_type=f32
+            nl[...], nr[p // 2, start:start + 2 * rows, :], (((1,), (1,)), ((), ())),
+            preferred_element_type=f32,
         ).astype(bf16).reshape(n, rows, 2 * rows)
-        if p == half - 1:
-            for d in range(n):
-                send(ksend.at[p], klast.at[x], ssem.at[8], lastsem, dev(xp(d), 1 - c, y, z))
-            return
         for d in range(1, n):
             send(ksend.at[p, xp(d)], arecv.at[p, d - 1], ssem.at[6], asem.at[p], dev(xp(d), c, y, z))
+
+    def last(k):
+        start = (2 + k) * rows
+        normalize(zp(1 - half) if k == 0 else zp(half), half // 2 - 1, start)
+        klast[k] = lax.dot_general(
+            nr[half // 2 - 1, start:start + rows, :], nl[...], (((1,), (1,)), ((), ())),
+            preferred_element_type=f32,
+        ).astype(bf16)
+        for d in range(n):
+            send(klast.at[k], kall.at[k, x], ssem.at[8], lastsem.at[k], dev(xp(d), 1 - c, y, z))
 
     def reduce(p):
         place = pl.ds((p % 2) * 2 * rows, 2 * rows)
@@ -230,27 +236,33 @@
         ).reshape(n, rows, width)
 
     def finish(p):
-        k = p % 2
-        if k == 0:
-            arrive(kfull.at[p // 2, :, :, pl.ds(0, 2 * rows)], dsem.at[p // 2])
-            s = kfull[p // 2, :, :, 0:2 * rows]
+        here = half // 2 - 1
+        if p == half - 2:
+            arrive(kfull.at[here, :, :, pl.ds(0, 2 * rows)], dsem.at[here])
+            product = jnp.dot(
+                kfull[here, :, :, 0:2 * rows].reshape(group, 2 * rows), nr[here, 0:2 * rows, :],
+                preferred_element_type=f32,
+            )
         else:
-            arrive(klast, lastsem)
-            s = klast[0].astype(f32)
-            for d in range(1, n):
-                s += klast[d].astype(f32)
-            s = s.astype(bf16)
-        acc[...] += jnp.dot(
-            s.reshape(group, 2 * rows), nr[p // 2, k * 2 * rows:(k + 1) * 2 * rows, :],
-            preferred_element_type=f32,
-        ).reshape(n, rows, width)
+            parts = []
+            for k in range(2):
+                arrive(kall.at[k], lastsem.at[k])
+                v = kall[k, 0].astype(f32)
+                for d in range(1, n):
+                    v += kall[k, d].astype(f32)
+                parts.append(v.astype(bf16))
+            product = lax.dot_general(
+                jnp.concatenate(parts, axis=0), nr[here, 2 * rows:4 * rows, :],
+                (((0,), (0,)), ((), ())), preferred_element_type=f32,
+            )
+        acc[...] += product.reshape(n, rows, width)
 
     for work, p in (
         (ring, 8), (multiply, 0), (ring, 9), (multiply, 1), (ring, 10), (multiply, 2),
         (ring, 11), (multiply, 3), (reduce, 0), (ring, 12), (reduce, 1), (ring, 13),
         (multiply, 4), (multiply, 5), (ring, 14), (reduce, 2), (reduce, 3), (ring, 15),
-        (multiply, 6), (consume, 0), (reduce, 4), (ring, 16), (ring, 17), (multiply, 7),
-        (reduce, 5), (reduce, 6), (consume, 1), (consume, 2), (finish, 6), (finish, 7),
+        (multiply, 6), (last, 0), (consume, 0), (reduce, 4), (reduce, 5), (ring, 16), (ring, 17),
+        (last, 1), (reduce, 6), (consume, 1), (consume, 2), (finish, 6), (finish, 7),
     ):
         work(p)
 
@@ -328,9 +340,9 @@
     arrive(lraw.at[pl.ds(0, n - 1)], ssem.at[3])
     arrive(stz.at[pl.ds(0, nz - 1)], ssem.at[4])
     arrive(mr.at[pl.ds(0, 2 * n - 1)], ssem.at[5])
-    arrive(arecv.at[pl.ds(0, half - 1)], ssem.at[6])
-    arrive(ksend.at[pl.ds(0, half - 1)], ssem.at[7])
-    arrive(klast, ssem.at[8])
+    arrive(arecv, ssem.at[6])
+    arrive(ksend, ssem.at[7])
+    arrive(kall, ssem.at[8])
     arrive(tl.at[pl.ds(0, nz - 1)], ssem.at[9])
     arrive(yrecv.at[pl.ds(0, 2 * n - 1)], ssem.at[10])
     arrive(ty.at[pl.ds(0, 2 * n - 1)], ssem.at[11])
@@ -363,11 +375,12 @@
             pltpu.VMEM((nz, 5, LANE), f32),
             pltpu.VMEM((2 * n, 5, LANE), f32),
             pltpu.VMEM((8, width), f32),
-            pltpu.VMEM((half, n, rows, 2 * rows), bf16),
-            pltpu.VMEM((half, n - 1, rows, 2 * rows), bf16),
-            pltpu.VMEM((half, rows, 2 * rows), bf16),
+            pltpu.VMEM((half - 1, n, rows, 2 * rows), bf16),
+            pltpu.VMEM((half - 1, n - 1, rows, 2 * rows), bf16),
+            pltpu.VMEM((half - 1, rows, 2 * rows), bf16),
             pltpu.VMEM((half // 2, n, rows, 4 * rows), bf16),
-            pltpu.VMEM((n, n, rows, 2 * rows), bf16),
+            pltpu.VMEM((2, rows, group), bf16),
+            pltpu.VMEM((2, n, rows, group), bf16),
             pltpu.VMEM((n, rows, width), f32),
             pltpu.VMEM((nz, 2, width), f32),
             pltpu.VMEM((2, 2, COLS), f32),
@@ -376,7 +389,7 @@
             pltpu.VMEM((2 * n, rows, COLS), bf16),
             pltpu.VMEM((8, COLS), f32),
             pltpu.VMEM((2 * n * n, 1, LANE), f32),
-            dma((13,)), dma((9,)), dma((2, half, PIECES)), dma((half,)), dma((half,)), dma((2,)), dma,
+            dma((13,)), dma((9,)), dma((2, half, PIECES)), dma((half,)), dma((half,)), dma((2,)), dma((2,)),
         ],
         compiler_params=pltpu.CompilerParams(
             collective_id=0, has_side_effects=True, vmem_limit_bytes=40 * 2**20

time: 72.2 us -> 70.5 us (0.976)
  Pallas kernels: 67.2 us -> 65.5 us
    pallas_call x1, Pallas kernels: 67.2 us -> 65.5 us  [local(): pl.pallas_call(kernel, out_shape=(jax.ShapeDtypeStruct(shape, bf16), jax....]
where the time goes in v5:
time: 70.5 us; the launch traced here: 70.3 us
  Pallas kernels  65.5 us (93%)
  local copies, waits for them, and re-layouts  2.93 us (4%)
  between operations  1.81 us (3%)
    pallas_call x1, Pallas kernels, local(): pl.pallas_call(kernel, out_shape=(jax.ShapeDtypeStruct(shape, bf16), jax....  65.5 us
    unnamed x6, local copies, waits for them, and re-layouts  2.93 us

profile of v5, /device:TPU:1, one launch (start us, length us, event | category | flops | bytes accessed | tf_op | source)
XLA Modules:
  0.0 70.3 jit_solution(7234974243866885819)
XLA Ops:
  0.6 0.0 copy-start
  0.6 0.8 %copy-done = bf16[64,512]{1,0:T(8,128)(2,1)S(1)} copy-done((bf16[64,512]{1,0:T(8,128)(2,1)S(1)}, bf16[64,512]{1,0:T(8,128)(2,1)}, u32[]{:S(2)}) %copy-start) | copy-done | bytes 65560
  1.5 0.0 copy-start.1
  1.5 0.8 %copy-done.1 = bf16[64,512]{1,0:T(8,128)(2,1)S(1)} copy-done((bf16[64,512]{1,0:T(8,128)(2,1)S(1)}, bf16[64,512]{1,0:T(8,128)(2,1)}, u32[]{:S(2)}) %copy-start.1) | copy-done | bytes 65560
  2.3 65.5 %shard_map.49 = (bf16[64,512]{1,0:T(8,128)(2,1)S(1)}, bf16[64,512]{1,0:T(8,128)(2,1)S(1)}, f32[1,128]{1,0:T(1,128)S(1)}) custom-call(bf16[64,512]{1,0:T(8,128)(2,1)S(1)} %copy-done, bf16[64,512]{1,0:T(8,128)(2,1)S(1)} %copy-done.1), custom_call_target="tpu_custom_call" | custom-call | tf_op jit(solution)/shard_map/pallas_call | solution.py:358
  67.8 0.6 copy.8
  68.5 0.6 copy.9
Async XLA Ops:
  0.6 0.8 %copy-start = (bf16[64,512]{1,0:T(8,128)(2,1)S(1)}, bf16[64,512]{1,0:T(8,128)(2,1)}, u32[]{:S(2)}) copy-start(bf16[64,512]{1,0:T(8,128)(2,1)} %x1.1) | copy-start | bytes 196612
  1.5 0.8 %copy-start.1 = (bf16[64,512]{1,0:T(8,128)(2,1)S(1)}, bf16[64,512]{1,0:T(8,128)(2,1)}, u32[]{:S(2)}) copy-start(bf16[64,512]{1,0:T(8,128)(2,1)} %x2.1) | copy-start | bytes 196612

commit v6 on v5

--- a/solution.py
+++ b/solution.py
@@ -58,13 +58,14 @@
         pltpu.make_async_copy(ref, ref, sem).wait()
 
     far = sorted(range(1, nz), key=lambda d: -min(d, nz - d))
+    side = sorted(range(n), key=lambda d: -min(d, n - d))
 
     barrier = pltpu.get_barrier_semaphore()
     peers = 0
     for d in far:
         pl.semaphore_signal(barrier, 1, device_id=dev(x, c, y, zp(d)), device_id_type=MESH)
         peers += 1
-    plane = [(dx, dc, dy) for dx in range(n) for dc in range(2) for dy in range(n)][1:]
+    plane = [(dx, dc, dy) for dx in side for dy in side for dc in (1, 0)][:-1]
     for dx, dc, dy in plane:
         to = dev(xp(dx), lax.rem(c + dc, 2), yp(dy), z)
         pl.semaphore_signal(barrier, 1, device_id=to, device_id_type=MESH)
@@ -123,7 +124,7 @@
     for i in range(np):
         for way in range(2):
             forward(way, 0, i)
-    for d in range(1, n):
+    for d in side[:-1]:
         send(stl.at[yp(d)], sty.at[y], ssem.at[1], misc.at[1], dev(x, c, yp(d), z))
     arrive(own.at[0, 0], misc.at[0])
     for r in range(np):
@@ -164,10 +165,9 @@
     mine = c * n + y
     for r, v in enumerate((m1, m2, i1, i2, s12 * i1 * i2 / all_rows)):
         mr[mine, r:r + 1, :] = v
-    for dc in range(2):
-        for d in range(n):
-            if d or dc:
-                send(mr.at[mine], mr.at[mine], ssem.at[5], misc.at[4], dev(x, lax.rem(c + dc, 2), yp(d), z))
+    row = [(dc, d) for d in side for dc in (1, 0)][:-1]
+    for dc, d in row:
+        send(mr.at[mine], mr.at[mine], ssem.at[5], misc.at[4], dev(x, lax.rem(c + dc, 2), yp(d), z))
     ring(2 * RING - 2)
     ring(2 * RING - 1)
     arrive(mr.at[pl.ds(0, 2 * n - 1)], misc.at[4])
@@ -203,7 +203,7 @@
             nl[...], nr[p // 2, start:start + 2 * rows, :], (((1,), (1,)), ((), ())),
             preferred_element_type=f32,
         ).astype(bf16).reshape(n, rows, 2 * rows)
-        for d in range(1, n):
+        for d in side[:-1]:
             send(ksend.at[p, xp(d)], arecv.at[p, d - 1], ssem.at[6], asem.at[p], dev(xp(d), c, y, z))
 
     def last(k):
@@ -213,7 +213,7 @@
             nr[half // 2 - 1, start:start + rows, :], nl[...], (((1,), (1,)), ((), ())),
             preferred_element_type=f32,
         ).astype(bf16)
-        for d in range(n):
+        for d in side:
             send(klast.at[k], kall.at[k, x], ssem.at[8], lastsem.at[k], dev(xp(d), 1 - c, y, z))
 
     def reduce(p):
@@ -223,7 +223,7 @@
         for d in range(n - 1):
             s += arecv[p, d].astype(f32)
         dsend[p] = s.astype(bf16)
-        for d in range(n):
+        for d in side:
             send(
                 dsend.at[p], kfull.at[p // 2, x, :, place], ssem.at[7], dsem.at[p // 2],
                 dev(xp(d), 1 - c, y, z),
@@ -279,7 +279,6 @@
     for q in range(n):
         for h in range(2):
             ysend[q, h] = acc[q, :, h * COLS:(h + 1) * COLS].astype(bf16)
-    row = [(dc, d) for dc in range(2) for d in range(n)][1:]
     for dc, d in row:
         cc, yy = lax.rem(c + dc, 2), yp(d)
         send(ysend.at[yy, cc], yrecv.at[c * n + y], ssem.at[10], misc.at[6], dev(x, cc, yy, z))

time: 70.5 us -> 69.7 us (0.989)
    pallas_call x1, Pallas kernels: 65.5 us -> 64.8 us  [local(): pl.pallas_call(kernel, out_shape=(jax.ShapeDtypeStruct(shape, bf16), jax....]
where the time goes in v6:
time: 69.7 us; the launch traced here: 69.5 us
  Pallas kernels  64.8 us (93%)
  local copies, waits for them, and re-layouts  2.93 us (4%)
  between operations  1.81 us (3%)
    pallas_call x1, Pallas kernels, local(): pl.pallas_call(kernel, out_shape=(jax.ShapeDtypeStruct(shape, bf16), jax....  64.8 us
    unnamed x6, local copies, waits for them, and re-layouts  2.93 us

profile of v6, /device:TPU:1, one launch (start us, length us, event | category | flops | bytes accessed | tf_op | source)
XLA Modules:
  0.0 69.5 jit_solution(5042278216122525510)
XLA Ops:
  0.6 0.0 copy-start
  0.6 0.8 %copy-done = bf16[64,512]{1,0:T(8,128)(2,1)S(1)} copy-done((bf16[64,512]{1,0:T(8,128)(2,1)S(1)}, bf16[64,512]{1,0:T(8,128)(2,1)}, u32[]{:S(2)}) %copy-start) | copy-done | bytes 65560
  1.5 0.0 copy-start.1
  1.5 0.8 %copy-done.1 = bf16[64,512]{1,0:T(8,128)(2,1)S(1)} copy-done((bf16[64,512]{1,0:T(8,128)(2,1)S(1)}, bf16[64,512]{1,0:T(8,128)(2,1)}, u32[]{:S(2)}) %copy-start.1) | copy-done | bytes 65560
  2.3 64.8 %shard_map.49 = (bf16[64,512]{1,0:T(8,128)(2,1)S(1)}, bf16[64,512]{1,0:T(8,128)(2,1)S(1)}, f32[1,128]{1,0:T(1,128)S(1)}) custom-call(bf16[64,512]{1,0:T(8,128)(2,1)S(1)} %copy-done, bf16[64,512]{1,0:T(8,128)(2,1)S(1)} %copy-done.1), custom_call_target="tpu_custom_call" | custom-call | tf_op jit(solution)/shard_map/pallas_call | solution.py:357
  67.1 0.6 copy.8
  67.7 0.6 copy.9
Async XLA Ops:
  0.6 0.8 %copy-start = (bf16[64,512]{1,0:T(8,128)(2,1)S(1)}, bf16[64,512]{1,0:T(8,128)(2,1)}, u32[]{:S(2)}) copy-start(bf16[64,512]{1,0:T(8,128)(2,1)} %x1.1) | copy-start | bytes 196612
  1.5 0.8 %copy-start.1 = (bf16[64,512]{1,0:T(8,128)(2,1)S(1)}, bf16[64,512]{1,0:T(8,128)(2,1)}, u32[]{:S(2)}) copy-start(bf16[64,512]{1,0:T(8,128)(2,1)} %x2.1) | copy-start | bytes 196612

commit v7 on v6

--- a/solution.py
+++ b/solution.py
@@ -21,7 +21,7 @@
 def kernel(
     x1, x2, o1, o2, loss_ref,
     own, gath, lraw, nl, nr, stl, sty, stz, mr, coef,
-    ksend, arecv, dsend, kfull, klast, kall, acc, tl, tsend, ty, ysend, yrecv, params, lbx,
+    ksend, arecv, dsend, kfull, klast, kall, acc, tl, tsend, ty, ysend, yrecv, params, hats, back, lbx,
     ssem, misc, grecv, asem, dsem, lsem, lastsem,
 ):
     n, nz, rows = SIDE, DEPTH, ROWS
@@ -283,6 +283,19 @@
         cc, yy = lax.rem(c + dc, 2), yp(d)
         send(ysend.at[yy, cc], yrecv.at[c * n + y], ssem.at[10], misc.at[6], dev(x, cc, yy, z))
     yrecv[c * n + y] = ysend[y, c]
+    scale = 2.0 * off_weight / all_rows
+    for q in range(n):
+        cols = slice(q * LANE, (q + 1) * LANE)
+        for r in range(5):
+            params[r:r + 1, cols] = mr[c * n + q, r:r + 1, :]
+    params[5:6, :] = -2.0 * (1.0 - params[4:5, :]) - 2.0 * off_weight * params[4:5, :]
+    params[6:7, :] = params[5:6, :] * params[4:5, :]
+    for v in range(2):
+        hats[v] = (own[v, c].astype(f32) - params[v:v + 1, :]) * params[2 + v:3 + v, :]
+    diagonal = coef[2:3, :]
+    coef[3:4, :] = (
+        (1.0 - diagonal) * (1.0 - diagonal) - off_weight * diagonal * diagonal
+    ) / n
     arrive(tl.at[pl.ds(0, nz - 1)], misc.at[5])
     sums = tl[0]
     for q in range(1, nz):
@@ -293,10 +306,7 @@
         cc, yy = lax.rem(c + dc, 2), yp(d)
         send(tsend.at[cc], ty.at[c * n + y], ssem.at[11], misc.at[7], dev(x, cc, yy, z))
     ty[c * n + y] = tsend[c]
-    diagonal = coef[2:3, :]
-    terms = ((1.0 - diagonal) * (1.0 - diagonal) - off_weight * diagonal * diagonal) / n + (
-        off_weight / (all_rows * all_rows)
-    ) * sums[1:2, :]
+    terms = coef[3:4, :] + (off_weight / (all_rows * all_rows)) * sums[1:2, :]
     place = t * n + y
     lbx[place] = jnp.broadcast_to(
         jnp.sum(terms, axis=1, keepdims=True) * (0.5 / features), (1, LANE)
@@ -305,27 +315,19 @@
         to = dev(xp(dx), lax.rem(c + dc, 2), yp(dy), z)
         send(lbx.at[place], lbx.at[place], ssem.at[12], misc.at[8], to)
 
-    scale = 2.0 * off_weight / all_rows
-    for q in range(n):
-        cols = slice(q * LANE, (q + 1) * LANE)
-        for r in range(5):
-            params[r:r + 1, cols] = mr[c * n + q, r:r + 1, :]
-    diagonal = params[4:5, :]
-    lead = -2.0 * (1.0 - diagonal) - 2.0 * off_weight * diagonal
-    hats = [
-        (own[v, c].astype(f32) - params[v:v + 1, :]) * params[2 + v:3 + v, :] for v in range(2)
-    ]
     arrive(yrecv.at[pl.ds(0, 2 * n - 1)], misc.at[6])
+    for v in range(2):
+        product = yrecv[v * n].astype(f32)
+        for q in range(1, n):
+            product += yrecv[v * n + q].astype(f32)
+        back[v] = scale * product + params[5:6, :] * hats[1 - v]
     arrive(ty.at[pl.ds(0, 2 * n - 1)], misc.at[7])
     for v, out in enumerate((o1, o2)):
-        product = yrecv[v * n].astype(f32)
         sums = ty[v * n]
         for q in range(1, n):
-            product += yrecv[v * n + q].astype(f32)
             sums += ty[v * n + q]
         sums = sums * (scale / all_rows)
-        back = scale * product + lead * hats[1 - v]
-        g = back - sums[0:1, :] - hats[v] * (sums[1:2, :] + lead * diagonal)
+        g = back[v] - sums[0:1, :] - hats[v] * (sums[1:2, :] + params[6:7, :])
         out[...] = (g * params[2 + v:3 + v, :]).astype(bf16)
     arrive(lbx.at[pl.ds(0, 2 * n * n - 1)], misc.at[8])
     part = lbx[0]
@@ -387,6 +389,8 @@
             pltpu.VMEM((n, 2, rows, COLS), bf16),
             pltpu.VMEM((2 * n, rows, COLS), bf16),
             pltpu.VMEM((8, COLS), f32),
+            pltpu.VMEM((2, rows, COLS), f32),
+            pltpu.VMEM((2, rows, COLS), f32),
             pltpu.VMEM((2 * n * n, 1, LANE), f32),
             dma((13,)), dma((9,)), dma((2, half, PIECES)), dma((half,)), dma((half,)), dma((2,)), dma((2,)),
         ],

time: 69.7 us -> 69.7 us (level)
  no operation moved by 1% of the time
where the time goes in v7:
time: 69.7 us; the launch traced here: 69.5 us
  Pallas kernels  64.8 us (93%)
  local copies, waits for them, and re-layouts  2.93 us (4%)
  between operations  1.81 us (3%)
    pallas_call x1, Pallas kernels, local(): pl.pallas_call(kernel, out_shape=(jax.ShapeDtypeStruct(shape, bf16), jax....  64.8 us
    unnamed x6, local copies, waits for them, and re-layouts  2.93 us

profile of v7, /device:TPU:1, one launch (start us, length us, event | category | flops | bytes accessed | tf_op | source)
XLA Modules:
  0.0 69.5 jit_solution(16273605776943089297)
XLA Ops:
  0.6 0.0 copy-start
  0.6 0.8 %copy-done = bf16[64,512]{1,0:T(8,128)(2,1)S(1)} copy-done((bf16[64,512]{1,0:T(8,128)(2,1)S(1)}, bf16[64,512]{1,0:T(8,128)(2,1)}, u32[]{:S(2)}) %copy-start) | copy-done | bytes 65560
  1.5 0.0 copy-start.1
  1.5 0.8 %copy-done.1 = bf16[64,512]{1,0:T(8,128)(2,1)S(1)} copy-done((bf16[64,512]{1,0:T(8,128)(2,1)S(1)}, bf16[64,512]{1,0:T(8,128)(2,1)}, u32[]{:S(2)}) %copy-start.1) | copy-done | bytes 65560
  2.3 64.8 %shard_map.49 = (bf16[64,512]{1,0:T(8,128)(2,1)S(1)}, bf16[64,512]{1,0:T(8,128)(2,1)S(1)}, f32[1,128]{1,0:T(1,128)S(1)}) custom-call(bf16[64,512]{1,0:T(8,128)(2,1)S(1)} %copy-done, bf16[64,512]{1,0:T(8,128)(2,1)S(1)} %copy-done.1), custom_call_target="tpu_custom_call" | custom-call | tf_op jit(solution)/shard_map/pallas_call | solution.py:359
  67.1 0.6 copy.8
  67.7 0.6 copy.9
Async XLA Ops:
  0.6 0.8 %copy-start = (bf16[64,512]{1,0:T(8,128)(2,1)S(1)}, bf16[64,512]{1,0:T(8,128)(2,1)}, u32[]{:S(2)}) copy-start(bf16[64,512]{1,0:T(8,128)(2,1)} %x1.1) | copy-start | bytes 196612
  1.5 0.8 %copy-start.1 = (bf16[64,512]{1,0:T(8,128)(2,1)S(1)}, bf16[64,512]{1,0:T(8,128)(2,1)}, u32[]{:S(2)}) copy-start(bf16[64,512]{1,0:T(8,128)(2,1)} %x2.1) | copy-start | bytes 196612
